TPU v7x, 512 devices: a whole 4x4x16 slice. The times are simulated.
512 devices in a mesh: lat: 8 (over z_hi, core), lon: 16 (over y, x), tp: 4 (over z_lo).
Axes of the slice: x: 4, y: 4, z: 16 (z_hi: 4, z_lo: 4; z = z_hi * 4 + z_lo), core: 2. Of those that a mesh axis runs over, the one named last changes fastest.
Arguments:
- fields: bfloat16 [128, 256, 1536], P('lat', 'lon', 'tp'), may hold values from -6 to 6
- w_qkv: bfloat16 [1536, 3, 768], P(None, None, 'tp'), may hold values from -0.15625 to 0.15625
- w_out: bfloat16 [768, 1536], P('tp'), may hold values from -0.21875 to 0.21875
- log_scale: float32 [12], P('tp'), may hold values from 0.7 to 3.4
- bias_table: float32 [225, 12], P(None, 'tp'), may hold values from -6 to 6
- bias_index: int32 [64, 64], replicated, may hold values from 0 to 224
- mask_ids: int32 [128, 256], P('lat', 'lon'), may hold values from 0 to 2
- norm_gain: float32 [1536], P('tp'), may hold values from 0.1 to 1.9
- norm_shift: float32 [1536], P('tp'), may hold values from -2 to 2
- cotangent: bfloat16 [128, 256, 1536], P('lat', 'lon', 'tp'), may hold values from -6 to 6
Outputs:
- block_out: bfloat16 [128, 256, 1536], P('lat', 'lon', 'tp')
- grad_fields: bfloat16 [128, 256, 1536], P('lat', 'lon', 'tp')
- grad_w_out: bfloat16 [768, 1536], P('tp')
- grad_table: float32 [225, 12], P(None, 'tp')
- grad_scale: float32 [12], P('tp')
- grad_gain: float32 [1536], P('tp')
- grad_shift: float32 [1536], P('tp')
Inputs may be any that keep to these rules, and one draw needn't show every extreme that they name: `bias_index`: each entry names a row of bias_table. `mask_ids`: two cells of one shifted window attend to each other only when their labels are equal.
All inputs are finite; a program needn't handle non-finite values.
Results may differ from a plain program's by a relative error of at most 0.02.
Values may be sent and summed in bfloat16 or wider, within the bound.
A program may use at most 64 MiB of HBM per device.

v0:
```python
import jax
import jax.numpy as jnp
from jax import lax
from jax.sharding import PartitionSpec as P

WIN = 8
SHIFT = 4


def shifted_2(value, axis, by):
    count = lax.axis_size(axis)
    return lax.ppermute(value, axis, [(i, (i + by) % count) for i in range(count)])


def mult(spec, left, right):
    return jnp.einsum(spec, left, right, preferred_element_type=jnp.float32)


def to_windows(tensor):
    extent_a, extent_b, heads_n, feature = tensor.shape
    tensor = tensor.reshape(extent_a // WIN, WIN, extent_b // WIN, WIN, heads_n, feature)
    tensor = tensor.transpose(0, 2, 4, 1, 3, 5)
    return tensor.reshape(extent_a // WIN * (extent_b // WIN), heads_n, WIN * WIN, feature)


def from_windows(tensor, extent_a, extent_b):
    n_windows, heads_n, win_cells, feature = tensor.shape
    tensor = tensor.reshape(extent_a // WIN, extent_b // WIN, heads_n, WIN, WIN, feature)
    tensor = tensor.transpose(0, 3, 1, 4, 2, 5)
    return tensor.reshape(extent_a, extent_b, heads_n * feature)


def window_ids(labels):
    extent_a, extent_b = labels.shape
    labels = labels.reshape(extent_a // WIN, WIN, extent_b // WIN, WIN).transpose(0, 2, 1, 3)
    return labels.reshape(-1, WIN * WIN)


def window_forward(proj_grid, log_scale, bias_sig, same_id):
    query = to_windows(proj_grid[:, :, 0])
    keys = to_windows(proj_grid[:, :, 1])
    values = to_windows(proj_grid[:, :, 2]).astype(jnp.bfloat16)
    q_len = jnp.sqrt(jnp.sum(query * query, -1, keepdims=True) + 1e-06)
    k_len = jnp.sqrt(jnp.sum(keys * keys, -1, keepdims=True) + 1e-06)
    q_hat = (query / q_len).astype(jnp.bfloat16)
    k_hat = (keys / k_len).astype(jnp.bfloat16)
    scale = jnp.exp(log_scale)[None, :, None, None]
    cosine = mult("nhie,nhje->nhij", q_hat, k_hat)
    logits = scale * cosine + 16.0 * bias_sig[None]
    weight = jnp.where(same_id, jnp.exp(logits - scale - 16.0), jnp.float32(0.0))
    prob = (weight / jnp.sum(weight, -1, keepdims=True)).astype(jnp.bfloat16)
    attended = mult("nhij,nhje->nhie", prob, values).astype(jnp.bfloat16)
    return (attended, (q_hat, k_hat, values, q_len, k_len, cosine, prob))


def window_backward(grad_grid, saved, log_scale, bias_sig):
    q_hat, k_hat, values, q_len, k_len, cosine, prob = saved
    extent_a, extent_b = (grad_grid.shape[0], grad_grid.shape[1])
    grad_att = to_windows(grad_grid)
    prob_f = prob.astype(jnp.float32)
    grad_prob = mult("nhie,nhje->nhij", grad_att, values)
    grad_logit = prob_f * (grad_prob - jnp.sum(prob_f * grad_prob, -1, keepdims=True))
    grad_values = mult("nhij,nhie->nhje", prob, grad_att).astype(jnp.bfloat16)
    table_terms = jnp.sum(grad_logit, 0) * 16.0 * bias_sig * (1.0 - bias_sig)
    scale_terms = jnp.sum(grad_logit * cosine, (0, 2, 3)) * jnp.exp(log_scale)
    scale = jnp.exp(log_scale)[None, :, None, None]
    grad_cos = (grad_logit * scale).astype(jnp.bfloat16)
    grad_qhat = mult("nhij,nhje->nhie", grad_cos, k_hat)
    grad_khat = mult("nhij,nhie->nhje", grad_cos, q_hat)
    q_float = q_hat.astype(jnp.float32)
    k_float = k_hat.astype(jnp.float32)
    grad_query = (
        (grad_qhat - q_float * jnp.sum(q_float * grad_qhat, -1, keepdims=True)) / q_len
    ).astype(jnp.bfloat16)
    grad_key = (
        (grad_khat - k_float * jnp.sum(k_float * grad_khat, -1, keepdims=True)) / k_len
    ).astype(jnp.bfloat16)
    stacked = jnp.stack(
        [
            from_windows(grad_query, extent_a, extent_b),
            from_windows(grad_key, extent_a, extent_b),
            from_windows(grad_values, extent_a, extent_b),
        ],
        2,
    )
    return (stacked, table_terms, scale_terms)


def into_window(tensor):
    rim = shifted_2(tensor[:SHIFT], "lat", -1)
    extended = jnp.concatenate([tensor[SHIFT:], rim], 0)
    side = shifted_2(extended[:, :SHIFT], "lon", -1)
    return jnp.concatenate([extended[:, SHIFT:], side], 1)


def out_of_window(tensor):
    rim = shifted_2(tensor[-SHIFT:].astype(jnp.bfloat16), "lat", 1).astype(jnp.float32)
    extended = jnp.concatenate([rim, tensor[:-SHIFT]], 0)
    side = shifted_2(extended[:, -SHIFT:].astype(jnp.bfloat16), "lon", 1).astype(jnp.float32)
    return jnp.concatenate([side, extended[:, :-SHIFT]], 1)


def per_device(
    fields,
    w_qkv,
    w_out,
    log_scale,
    bias_table,
    bias_index,
    mask_ids,
    norm_gain,
    norm_shift,
    cotangent,
):
    extent_a, extent_b, shard_chan = fields.shape
    channels = w_qkv.shape[0]
    att_width = w_out.shape[0]
    local_heads = log_scale.shape[0]
    head_size = att_width // local_heads
    n_cells = extent_a * extent_b
    first_chan = lax.axis_index("tp") * shard_chan
    w_flat = w_qkv.reshape(channels, 3 * att_width)
    shifted = into_window(fields)
    piece = lax.all_gather(shifted, "tp", axis=2, tiled=True)
    piece_len = piece.shape[2]
    block = w_flat
    proj = jnp.dot(piece.reshape(n_cells, piece_len), block, preferred_element_type=jnp.float32)
    proj = proj.reshape(extent_a, extent_b, 3, local_heads, head_size)
    table_size = bias_table.shape[0]
    one_hot = (
        bias_index.reshape(-1, 1) == jnp.arange(table_size, dtype=jnp.int32)[None, :]
    ).astype(jnp.float32)
    bias_values = jnp.dot(one_hot, bias_table, precision=lax.Precision.HIGHEST)
    bias_sig = (
        jax.nn.sigmoid(bias_values).reshape(WIN * WIN, WIN * WIN, local_heads).transpose(2, 0, 1)
    )
    labels = window_ids(mask_ids)
    same_id = (labels[:, :, None] == labels[:, None, :])[:, None]
    attended, saved = window_forward(proj, log_scale, bias_sig, same_id)
    att_grid = from_windows(attended, extent_a, extent_b).reshape(n_cells, att_width)
    head_terms = jnp.dot(att_grid, w_out, preferred_element_type=jnp.float32)
    whole = lax.psum(head_terms.astype(jnp.bfloat16), "tp").astype(jnp.float32)
    row_sum = jnp.sum(whole, 1, keepdims=True)
    row_squares = jnp.sum(whole * whole, 1, keepdims=True)
    mixed = lax.dynamic_slice_in_dim(whole, first_chan, shard_chan, 1)
    row_mean = row_sum / channels
    row_var = row_squares / channels - row_mean * row_mean
    inv_std = 1.0 / jnp.sqrt(row_var + 1e-05)
    normed = (mixed - row_mean) * inv_std
    branch = (norm_gain * normed + norm_shift).reshape(extent_a, extent_b, shard_chan)
    block_out = (fields.astype(jnp.float32) + out_of_window(branch)).astype(jnp.bfloat16)
    grad_rows = into_window(cotangent).reshape(n_cells, shard_chan).astype(jnp.float32)
    grad_norm = grad_rows * norm_gain
    sum_grad, sum_cross = lax.psum(
        (jnp.sum(grad_norm, 1, keepdims=True), jnp.sum(grad_norm * normed, 1, keepdims=True)), "tp"
    )
    grad_mixed = (
        inv_std * (grad_norm - sum_grad / channels - normed * (sum_cross / channels))
    ).astype(jnp.bfloat16)
    grad_mixed = grad_mixed.reshape(extent_a, extent_b, shard_chan)
    piece = lax.all_gather(grad_mixed, "tp", axis=2, tiled=True)
    piece_len = piece.shape[2]
    rows_flat = piece.reshape(n_cells, piece_len)
    block = w_out
    att_part = lax.dot_general(
        rows_flat, block, (((1,), (1,)), ((), ())), preferred_element_type=jnp.float32
    )
    weight_cols = lax.dot_general(
        att_grid, rows_flat, (((0,), (0,)), ((), ())), preferred_element_type=jnp.float32
    )
    grad_att = att_part
    grad_w_out = lax.psum(weight_cols, ("lat", "lon")).astype(jnp.bfloat16)
    grad_att = grad_att.astype(jnp.bfloat16).reshape(extent_a, extent_b, local_heads, head_size)
    stacked, table_terms, scale_terms = window_backward(grad_att, saved, log_scale, bias_sig)
    flat_terms = table_terms.transpose(1, 2, 0).reshape(-1, local_heads)
    table_local = lax.dot_general(
        one_hot, flat_terms, (((0,), (0,)), ((), ())), precision=lax.Precision.HIGHEST
    )
    grad_table, grad_scale, grad_gain, grad_shift = lax.psum(
        (table_local, scale_terms, jnp.sum(grad_rows * normed, 0), jnp.sum(grad_rows, 0)),
        ("lat", "lon"),
    )
    input_terms = lax.dot_general(
        stacked.reshape(n_cells, 3 * att_width),
        w_flat,
        (((1,), (1,)), ((), ())),
        preferred_element_type=jnp.float32,
    )
    grad_share = lax.psum_scatter(
        input_terms.astype(jnp.bfloat16), "tp", scatter_dimension=1, tiled=True
    ).astype(jnp.float32)
    grad_fields = (
        cotangent.astype(jnp.float32)
        + out_of_window(grad_share.reshape(extent_a, extent_b, shard_chan))
    ).astype(jnp.bfloat16)
    return (block_out, grad_fields, grad_w_out, grad_table, grad_scale, grad_gain, grad_shift)


def solution(mesh):
    in_specs = (
        P("lat", "lon", "tp"),
        P(None, None, "tp"),
        P("tp", None),
        P("tp"),
        P(None, "tp"),
        P(),
        P("lat", "lon"),
        P("tp"),
        P("tp"),
        P("lat", "lon", "tp"),
    )
    out_specs = (
        P("lat", "lon", "tp"),
        P("lat", "lon", "tp"),
        P("tp", None),
        P(None, "tp"),
        P("tp"),
        P("tp"),
        P("tp"),
    )
    return jax.shard_map(
        per_device, mesh=mesh, in_specs=in_specs, out_specs=out_specs, check_vma=False
    )
```

profile of v0, /device:TPU:1, one launch (start us, length us, event | category | flops | bytes accessed | tf_op | source)
XLA Modules:
  0.0 1048.8 jit_solution(13955392233251226195)
XLA Ops:
  7.3 0.9 slice.73
  8.2 8.8 collective-permute-start
  17.0 0.8 eq.38
  17.8 2.9 fusion.5
  21.4 5.6 collective-permute-start.1
  27.1 1.1 collective-permute-done.1
  28.2 17.6 %all_gather.6 = bf16[16,16,1536]{2,1,0:T(8,128)(2,1)S(1)} all-gather(bf16[16,16,384]{2,1,0:T(8,128)(2,1)S(1)} %pad_maximum_fusion.3), channel_id=1, replica_groups=mesh['lat'=8,'lon'=16,'tp'=4] {'tp'}, dimensions={2}, use_global_device_ids=true | all-gather | bytes 983040 | tf_op jit(solution)/shard_map/all_gather | solution.py:124
  45.8 1.2 fusion.19
  50.3 1.3 convolution_convert_fusion.1
  51.6 9.2 collective-permute-start.4
  60.9 1.6 collective-permute-done.4
  62.5 7.5 collective-permute-start.5
  70.1 1.1 collective-permute-done.5
  72.5 48.0 %all-reduce.5.cloned.1.call-done = bf16[256,1536]{1,0:T(8,128)(2,1)} async-done(((bf16[256,1536]{1,0:T(8,128)(2,1)}), bf16[256,1536]{1,0:T(8,128)(2,1)}) %all-reduce.5.cloned.1.call-update) | async-done | bytes 786448 | tf_op jit(solution)/shard_map/psum | solution.py:142
  120.5 1.5 convert_reduce_fusion
  122.0 1.3 convert_element_type.112
  123.4 0.8 fusion.34
  124.2 9.3 all-reduce.1
  133.5 0.7 broadcast_multiply_fusion.1
  134.9 1.8 fusion.31
  136.7 15.4 %all_gather.7 = bf16[16,16,1536]{2,1,0:T(8,128)(2,1)S(1)} all-gather(bf16[16,16,384]{2,1,0:T(8,128)(2,1)S(1)} %bitcast.142), channel_id=1, replica_groups=mesh['lat'=8,'lon'=16,'tp'=4] {'tp'}, dimensions={2}, use_global_device_ids=true | all-gather | bytes 983040 | tf_op jit(solution)/shard_map/all_gather | solution.py:161
  153.0 2.1 fusion.43
  155.1 2.0 fusion.42
  157.1 0.9 convolution_convert_fusion.2
  158.0 1.4 fusion.17
  159.9 1.4 fusion.18
  162.7 1.1 reshape.153
  163.8 2.6 convolution_convert_fusion
  166.5 2.4 copy.135
  168.9 0.7 multiply_reduce_fusion.1
  169.7 0.9 fusion.41
  170.8 0.9 slice.121
  171.8 11.9 %collective-permute-start.2 = (bf16[4,16,384]{2,1,0:T(8,128)(2,1)S(1)}, bf16[4,16,384]{2,1,0:T(8,128)(2,1)S(1)}, u32[]{:S(2)}, u32[]{:S(2)}) collective-permute-start(bf16[4,16,384]{2,1,0:T(8,128)(2,1)S(1)} %bitcast.146), channel_id=1, source_target_pairs={{0,64},{64,128},{128,192},{192,256},{256,320},{320,384},{384,448},... | collective-permute-start | bytes 147464 | tf_op jit(solution)/shard_map/ppermute | solution.py:12
  183.6 2.0 fusion.6
  185.6 1.4 fusion.46
  187.8 3.1 collective-permute-start.3
  190.9 14.1 %reduce-scatter.4.cloned.1.call-done = bf16[384,256]{1,0:T(8,128)(2,1)} async-done(((bf16[1536,256]{1,0:T(8,128)(2,1)}), bf16[384,256]{1,0:T(8,128)(2,1)}) %reduce-scatter.4.cloned.1.call-update) | async-done | bytes 196624
  205.0 1.6 slice.104
  206.6 1.6 copy.137
  208.2 9.2 collective-permute-start.6
  217.5 762.0 %all-reduce.6 = (bf16[192,1536]{1,0:T(8,128)(2,1)}, f32[225,3]{0,1:T(4,128)}, f32[3]{0:T(128)}, f32[384]{0:T(512)}, f32[384]{0:T(512)}) all-reduce(f32[192,1536]{1,0:T(8,128)S(1)} %copy-done.1, f32[225,3]{0,1:T(4,128)S(1)} %copy-done.34, f32[3]{0:T(128)S(1)} %exponential_multiply_fusion, ...), channel_id=1, replica_groups=mesh['lat'=8,'lon'=16,'tp'=4] {'lat','lon'}, use_global_device_ids=true, to_apply=%region_14.15 | all-reduce | flops 296358 | bytes 1781040 | tf_op jit(solution)/shard_map/psum | solution.py:172
  979.4 0.8 convert_element_type.115
  980.3 1.1 copy.138
  981.4 0.8 pad_maximum_fusion.5
  982.1 1.9 collective-permute-start.7
  984.1 0.8 fusion.26
  984.8 55.6 %collective-permute-done.7 = bf16[16,4,384]{2,1,0:T(4,128)(2,1)S(1)} collective-permute-done((bf16[16,4,384]{2,1,0:T(4,128)(2,1)S(1)}, bf16[16,4,384]{2,1,0:T(4,128)(2,1)S(1)}, u32[]{:S(2)}, u32[]{:S(2)}) %collective-permute-start.7) | collective-permute-done | bytes 49184 | tf_op jit(solution)/shard_map/ppermute | solution.py:12
  1040.4 1.6 add_convert_fusion
  (146 shorter events, 9.7 us)
Async XLA Ops:
  7.2 38.6 %copy-start = (bf16[1536,3,192]{0,2,1:T(8,128)(2,1)S(1)}, bf16[1536,3,192]{0,2,1:T(8,128)(2,1)}, u32[]{:S(2)}) copy-start(bf16[1536,3,192]{0,2,1:T(8,128)(2,1)} %param.11) | copy-start | bytes 5308420
  7.2 14.1 %copy-start.16 = (bf16[16,16,384]{2,1,0:T(8,128)(2,1)S(1)}, bf16[16,16,384]{2,1,0:T(8,128)(2,1)}, u32[]{:S(2)}) copy-start(bf16[16,16,384]{2,1,0:T(8,128)(2,1)} %param.10) | copy-start | bytes 589828
  7.2 13.8 %copy-start.33 = (s32[16,16]{1,0:T(8,128)S(1)}, s32[16,16]{1,0:T(8,128)}, u32[]{:S(2)}) copy-start(s32[16,16]{1,0:T(8,128)} %param.16) | copy-start | bytes 3076
  7.2 14.1 %copy-start.37 = (f32[3]{0:T(128)S(1)}, f32[3]{0:T(128)}, u32[]{:S(2)}) copy-start(f32[3]{0:T(128)} %param.13) | copy-start | bytes 40
  7.2 113.3 %all-reduce.5.cloned.1.call-start = ((), (), s32[]{:S(2)}) async-start(), calls=%async_computation.1 | async-start | bytes 1572864 | tf_op jit(solution)/shard_map/psum | solution.py:142
  8.2 13.2 %collective-permute-start = (bf16[4,16,384]{2,1,0:T(8,128)(2,1)S(1)}, bf16[4,16,384]{2,1,0:T(8,128)(2,1)S(1)}, u32[]{:S(2)}, u32[]{:S(2)}) collective-permute-start(bf16[4,16,384]{2,1,0:T(8,128)(2,1)S(1)} %slice.73), channel_id=1, source_target_pairs={{0,448},{64,0},{128,64},{192,128},{256,192},{320,256},{384,320},{4... | collective-permute-start | bytes 147464 | tf_op jit(solution)/shard_map/ppermute | solution.py:12
  17.8 2.9 copy-start.27
  21.0 26.0 %copy-start.15 = (f32[64,64,3]{0,1,2:T(8,128)}, f32[64,64,3]{0,1,2:T(8,128)S(1)}, u32[]{:S(2)}) copy-start(f32[64,64,3]{0,1,2:T(8,128)S(1)} %copy.110) | copy-start | bytes 147460
  21.3 27.3 %copy-start.35 = (f32[3]{0:T(128)}, f32[3]{0:T(128)S(1)}, u32[]{:S(2)}) copy-start(f32[3]{0:T(128)S(1)} %exp.11) | copy-start | bytes 40
  21.4 6.8 collective-permute-start.1
  48.2 1.7 copy-start.6
  48.3 1.6 copy-start.23
  48.3 2.0 copy-start.24
  48.3 1.9 copy-start.4
  48.7 1.2 copy-start.8
  49.9 1.8 copy-start.19
  50.3 19.8 %copy-start.13 = (bf16[256,192]{1,0:T(8,128)(2,1)}, bf16[256,192]{1,0:T(8,128)(2,1)S(1)}, u32[]{:S(2)}) copy-start(bf16[256,192]{1,0:T(8,128)(2,1)S(1)} %reshape_reshape.6) | copy-start | bytes 294916
  50.3 20.9 %copy-start.25 = (f32[384]{0:T(512)S(1)}, f32[384]{0:T(512)}, u32[]{:S(2)}) copy-start(f32[384]{0:T(512)} %param.17) | copy-start | bytes 4612
  51.6 153.4 %reduce-scatter.4.cloned.1.call-start = ((), (), s32[]{:S(2)}) async-start(), calls=%async_computation.2 | async-start | bytes 983040
  51.6 10.9 %collective-permute-start.4 = (bf16[4,16,384]{2,1,0:T(8,128)(2,1)S(1)}, bf16[4,16,384]{2,1,0:T(8,128)(2,1)S(1)}, u32[]{:S(2)}, u32[]{:S(2)}) collective-permute-start(bf16[4,16,384]{2,1,0:T(8,128)(2,1)S(1)} %slice.85), channel_id=1, source_target_pairs={{0,448},{64,0},{128,64},{192,128},{256,192},{320,256},{384,320},{4... | collective-permute-start | bytes 147464 | tf_op jit(solution)/shard_map/ppermute | solution.py:12
  62.5 8.6 collective-permute-start.5
  71.2 50.8 %copy-start.21 = (bf16[16,4,384]{2,1,0:T(4,128)(2,1)}, bf16[16,4,384]{2,1,0:T(4,128)(2,1)S(1)}, u32[]{:S(2)}) copy-start(bf16[16,4,384]{2,1,0:T(4,128)(2,1)S(1)} %collective-permute-done.5) | copy-start | bytes 147460
  120.5 2.9 copy-start.26
  122.0 2.2 copy-start.29
  122.0 2.2 copy-start.30
  122.0 1.3 copy-start.22
  133.5 18.6 %copy-start.5 = (bf16[192,1536]{1,0:T(8,128)(2,1)S(1)}, bf16[192,1536]{1,0:T(8,128)(2,1)}, u32[]{:S(2)}) copy-start(bf16[192,1536]{1,0:T(8,128)(2,1)} %param.12) | copy-start | bytes 1769476
  136.7 16.1 %copy-start.7 = (bf16[2,2,3,8,8,64]{5,4,3,2,1,0:T(8,128)(2,1)S(1)}, bf16[2,2,3,8,8,64]{5,4,3,2,1,0:T(8,128)(2,1)}, u32[]{:S(2)}) copy-start(bf16[2,2,3,8,8,64]{5,4,3,2,1,0:T(8,128)(2,1)} %copy-done.6) | copy-start | bytes 294916
  152.1 0.9 copy-start.3
  153.0 6.4 copy-start.10
  159.9 2.0 copy-start.18
  166.5 2.4 copy-start.9
  166.5 2.4 copy-start.11
  168.9 14.7 %copy-start.28 = (s32[4096]{0:T(1024)S(1)}, s32[4096]{0:T(1024)}, u32[]{:S(2)}) copy-start(s32[4096]{0:T(1024)} %copy-done.27) | copy-start | bytes 49156
  169.7 16.0 %copy-start.14 = (bf16[256,192]{1,0:T(8,128)(2,1)S(1)}, bf16[256,192]{1,0:T(8,128)(2,1)}, u32[]{:S(2)}) copy-start(bf16[256,192]{1,0:T(8,128)(2,1)} %copy-done.13) | copy-start | bytes 294916
  171.7 15.3 %copy-start.36 = (f32[3]{0:T(128)S(1)}, f32[3]{0:T(128)}, u32[]{:S(2)}) copy-start(f32[3]{0:T(128)} %get-tuple-element.11) | copy-start | bytes 40
  171.7 15.3 %copy-start.38 = (f32[3]{0:T(128)S(1)}, f32[3]{0:T(128)}, u32[]{:S(2)}) copy-start(f32[3]{0:T(128)} %param.13) | copy-start | bytes 40
  171.7 15.3 %copy-start.12 = (f32[256,384]{1,0:T(8,128)S(1)}, f32[256,384]{1,0:T(8,128)}, u32[]{:S(2)}) copy-start(f32[256,384]{1,0:T(8,128)} %get-tuple-element.23) | copy-start | bytes 1179652
  171.8 15.3 %collective-permute-start.2 = (bf16[4,16,384]{2,1,0:T(8,128)(2,1)S(1)}, bf16[4,16,384]{2,1,0:T(8,128)(2,1)S(1)}, u32[]{:S(2)}, u32[]{:S(2)}) collective-permute-start(bf16[4,16,384]{2,1,0:T(8,128)(2,1)S(1)} %bitcast.146), channel_id=1, source_target_pairs={{0,64},{64,128},{128,192},{192,256},{256,320},{320,384},{384,448},... | collective-permute-start | bytes 147464 | tf_op jit(solution)/shard_map/ppermute | solution.py:12
  185.6 31.8 %copy-start.31 = (f32[384]{0:T(512)S(1)}, f32[384]{0:T(512)}, u32[]{:S(2)}) copy-start(f32[384]{0:T(512)} %get-tuple-element.13) | copy-start | bytes 4612
  185.6 31.8 %copy-start.32 = (f32[384]{0:T(512)S(1)}, f32[384]{0:T(512)}, u32[]{:S(2)}) copy-start(f32[384]{0:T(512)} %get-tuple-element.7) | copy-start | bytes 4612
  185.6 31.8 %copy-start.34 = (f32[225,3]{0,1:T(4,128)S(1)}, f32[225,3]{0,1:T(4,128)}, u32[]{:S(2)}) copy-start(f32[225,3]{0,1:T(4,128)} %fusion.6) | copy-start | bytes 8104
  187.0 30.4 %copy-start.1 = (f32[192,1536]{1,0:T(8,128)S(1)}, f32[192,1536]{1,0:T(8,128)}, u32[]{:S(2)}) copy-start(f32[192,1536]{1,0:T(8,128)} %fusion.46) | copy-start | bytes 3538948
  187.1 797.0 %copy-start.17 = (bf16[16,16,384]{2,1,0:T(8,128)(2,1)S(1)}, bf16[16,16,384]{2,1,0:T(8,128)(2,1)}, u32[]{:S(2)}) copy-start(bf16[16,16,384]{2,1,0:T(8,128)(2,1)} %param.10) | copy-start | bytes 589828
  187.8 791.7 %collective-permute-start.3 = (bf16[16,4,384]{2,1,0:T(4,128)(2,1)}, bf16[16,4,384]{2,1,0:T(4,128)(2,1)}, u32[]{:S(2)}, u32[]{:S(2)}) collective-permute-start(bf16[16,4,384]{2,1,0:T(4,128)(2,1)} %fusion.40), channel_id=1, source_target_pairs={{0,4},{4,8},{8,12},{12,16},{16,20},{20,24},{24,28},{28,32},{32,36}... | collective-permute-start | bytes 147464 | tf_op jit(solution)/shard_map/ppermute | solution.py:12
  208.2 773.2 %collective-permute-start.6 = (bf16[4,16,384]{2,1,0:T(8,128)(2,1)}, bf16[4,16,384]{2,1,0:T(8,128)(2,1)}, u32[]{:S(2)}, u32[]{:S(2)}) collective-permute-start(bf16[4,16,384]{2,1,0:T(8,128)(2,1)} %bitcast.147), channel_id=1, source_target_pairs={{0,64},{64,128},{128,192},{192,256},{256,320},{320,384},{384,448},... | collective-permute-start | bytes 147464 | tf_op jit(solution)/shard_map/ppermute | solution.py:12
  979.4 61.0 %copy-start.20 = (bf16[16,16,384]{2,1,0:T(8,128)(2,1)S(1)}, bf16[16,16,384]{2,1,0:T(8,128)(2,1)}, u32[]{:S(2)}) copy-start(bf16[16,16,384]{2,1,0:T(8,128)(2,1)} %param.19) | copy-start | bytes 589828
  982.1 58.3 %collective-permute-start.7 = (bf16[16,4,384]{2,1,0:T(4,128)(2,1)S(1)}, bf16[16,4,384]{2,1,0:T(4,128)(2,1)S(1)}, u32[]{:S(2)}, u32[]{:S(2)}) collective-permute-start(bf16[16,4,384]{2,1,0:T(4,128)(2,1)S(1)} %pad_maximum_fusion.5), channel_id=1, source_target_pairs={{0,4},{4,8},{8,12},{12,16},{16,20},{20,24},{24,28},{28,32},{32,36}... | collective-permute-start | bytes 147464 | tf_op jit(solution)/shard_map/ppermute | solution.py:12
  (1 other events, 0.7 us)
Sparse Core Ops, SparseCore 0:
  51.7 68.7 all-reduce.4
  169.0 35.8 reduce-scatter.3
where the time goes:
time: 1050 us
  blocking collectives  804 us (77%)
  waiting for transfers between devices  122 us (12%)
  starting transfers between devices  57.2 us (5%)
  other arithmetic  17.7 us (2%)
  matrix products  17.6 us (2%)
  local copies, waits for them, and re-layouts  15.7 us (1%)
  between operations  14.9 us (1%)
    psum x1, blocking collectives, per_device(): grad_w_out = lax.psum(weight_cols, ('lat', 'lon')).astype(jnp.bfloat16)  762 us
    ppermute x8, waiting for transfers between devices, shifted_2(): lax.ppermute(value, axis, [(i, (i + by) % count) for i in range(count)])  59.4 us
    ppermute x8, starting transfers between devices, shifted_2(): lax.ppermute(value, axis, [(i, (i + by) % count) for i in range(count)])  57.1 us
    psum x1, waiting for transfers between devices, per_device(): whole = lax.psum(head_terms.astype(jnp.bfloat16), 'tp').astype(jnp.float32)  48 us
  transfers between devices with their start and end apart: 10, of which 6 were waited for; matrix products, arithmetic and copies ran while one was open for 2% of the time, Pallas kernels for 0%

commit v1 on v0

v1 whole, which is shorter than its diff:
```python
import jax
import jax.numpy as jnp
from jax import lax
from jax.experimental import pallas as pl
from jax.experimental.pallas import tpu as pltpu
from jax.sharding import PartitionSpec as P

MESH = pl.DeviceIdType.MESH
BF = jnp.bfloat16
F32 = jnp.float32

CH = 1536
SH = 384
HEADS = 3
HD = 64
AW = HEADS * HD
CELLS = 64
NWIN = 4
GROUPS = 2
WIN = 8
TABLE = 256
NPAIR = 4096

SLOTS = {}
COUNT = 0
for _name, _n in (
    ("halo_f", 5), ("halo_c", 5), ("fields", 16), ("wcol_z", 3), ("wcol_p", 15), ("att", 8), ("stat", 6),
    ("gatt", 8), ("gsh", 8), ("out_f", 5), ("out_g", 5), ("w_core", 1), ("w_p", 15), ("w_z", 16),
    ("w_zs", 8), ("back_p", 15), ("back_core", 12), ("s_p", 15), ("s_l", 7),
):
    SLOTS[_name] = COUNT
    COUNT += _n

PLANE = [(dy, dx) for dy in range(4) for dx in range(4)][1:]


def nn(a, b):
    return lax.dot_general(a, b, (((1,), (0,)), ((), ())), preferred_element_type=F32)


def nt(a, b):
    return lax.dot_general(a, b, (((1,), (1,)), ((), ())), preferred_element_type=F32)


def tn(a, b):
    return lax.dot_general(a, b, (((0,), (0,)), ((), ())), preferred_element_type=F32)


def split3(value):
    high = value.astype(BF).astype(F32)
    middle = (value - high).astype(BF).astype(F32)
    return high, middle, value - high - middle


def swap_halves(first, second):
    low = lax.broadcasted_iota(jnp.int32, first.shape, 0) < 4
    return jnp.where(low, first, pltpu.roll(second, 4, 0)), jnp.where(low, pltpu.roll(first, 4, 0), second)


def cut_blocks(grid, blocks):
    for i in range(4):
        tiles = [[None, None] for _ in range(4)]
        for half in (0, 1):
            upper = grid[4 * i + 2 * half].astype(F32)
            lower = grid[4 * i + 2 * half + 1].astype(F32)
            for k in (0, 1):
                pair = swap_halves(upper[8 * k:8 * k + 8], lower[8 * k:8 * k + 8])
                tiles[2 * k][half], tiles[2 * k + 1][half] = pair
        for j in range(4):
            blocks[i, j] = jnp.concatenate(tiles[j], axis=0).astype(BF)


def join_blocks(blocks, grid):
    for i in range(4):
        for half in (0, 1):
            upper, lower = [], []
            for k in (0, 1):
                rows = slice(8 * half, 8 * half + 8)
                pair = swap_halves(blocks[i, 2 * k].astype(F32)[rows], blocks[i, 2 * k + 1].astype(F32)[rows])
                upper.append(pair[0])
                lower.append(pair[1])
            grid[4 * i + 2 * half] = jnp.concatenate(upper, axis=0).astype(BF)
            grid[4 * i + 2 * half + 1] = jnp.concatenate(lower, axis=0).astype(BF)


def write_kernel(blocks_f, blocks_g, weights, small, out_f, out_g, out_w, out_t, out_s, out_a, out_b):
    out_w[...] = weights[...]
    join_blocks(blocks_f, out_f)
    join_blocks(blocks_g, out_g)
    out_t[...] = small[2:2 + HEADS, 0:out_t.shape[1]]
    spare = small[2:2 + HEADS, TABLE - 1:TABLE]
    scales = jnp.transpose(jnp.concatenate([jnp.broadcast_to(spare, (HEADS, 128)), jnp.zeros((8 - HEADS, 128), F32)], axis=0))
    out_s[...] = scales[0:1, 0:HEADS].reshape(HEADS)
    out_a[...] = small[0]
    out_b[...] = small[1]


def whole_kernel(
    fields_grid, cot_grid, wt, wout, logs, table, index, mask, gain_ref, shift_ref,
    out_f, out_g, out_w, out_s,
    fields, cot, xbuf, cbuf, wcol, abuf, onehot, bsrow, idx_row, tab_pad, bsig, lab_col, qs, ks, vs, probs, coss, rqs, rks,
    mixed, stat_all, gmix, ga_send, ga_recv, ga_relay, gs_send, gs_recv, gs_relay, obuf, gobuf, tacc, sacc, gacc, flat,
    wc_send, wc_recv, wacc, wp_send, wp_recv, wp_sum, bz, sm_p, sm_l, local_sem, ssem, rsem,
):
    lat = lax.axis_index("lat")
    lon = lax.axis_index("lon")
    t = lax.axis_index("tp")
    zh = lat // 2
    core = lat % 2
    ly = lon // 4
    lx = lon % 4

    def ring(value, by, count):
        return lax.rem(value + by + count, count)

    lat_p, lat_n = ring(lat, -1, 8), ring(lat, 1, 8)
    lon_p, lon_n = ring(lon, -1, 16), ring(lon, 1, 16)
    sib = (zh * 2 + (1 - core), lon, t)

    def tp_dev(d):
        return (lat, lon, ring(t, d, 4))

    def plane(o):
        return ring(ly, PLANE[o][0], 4), ring(lx, PLANE[o][1], 4)

    def plane_from(o):
        return ring(ly, -PLANE[o][0], 4), ring(lx, -PLANE[o][1], 4)

    def plane_dev(o):
        y, x = plane(o)
        return (lat, y * 4 + x, t)

    def z_dev(d):
        return (ring(zh, d, 4) * 2 + core, lon, t)

    def copy(src, dst, slot, dev, send_slot=None):
        return pltpu.make_async_remote_copy(
            src_ref=src, dst_ref=dst, send_sem=ssem.at[slot if send_slot is None else send_slot],
            recv_sem=rsem.at[slot], device_id=dev, device_id_type=MESH,
        )

    def send(src, dst, slot, dev, send_slot=None):
        copy(src, dst, slot, dev, send_slot).start()

    def got(dst, slot):
        copy(dst, dst, slot, sib).wait_recv()

    def sent(src, slot):
        copy(src, src, slot, sib).wait_send()

    partners = [plane_dev(o) for o in range(15)] + [(ring(lat, d, 8), lon, t) for d in range(1, 8)]
    partners += [(lat_p, lon_p, t), (lat_n, lon_n, t)] + [tp_dev(d) for d in (1, 2, 3)]
    partners += [(ring(zh, dz, 4) * 2 + core, lon, ring(t, dt, 4)) for dz in (1, 2, 3) for dt in (1, 2, 3)]
    barrier = pltpu.get_barrier_semaphore()
    for dev in partners:
        pl.semaphore_signal(barrier, inc=1, device_id=dev, device_id_type=MESH)

    own = []

    def keep(src, dst):
        own.append(pltpu.make_async_copy(src, dst, local_sem.at[len(own)]))
        own[-1].start()

    def keep_grid(grid, dst):
        keep(grid.at[1:3, 1:3], dst.at[0])
        keep(grid.at[1:3, 3], dst.at[1, :, 0])
        keep(grid.at[3, 1:3], dst.at[2, 0])
        keep(grid.at[3, 3], dst.at[3, 0, 0])

    x_own = xbuf.at[t]
    cut_blocks(fields_grid, fields)
    keep_grid(fields, x_own)

    pl.semaphore_wait(barrier, len(partners))

    def halo(grid, dst, base):
        send(grid.at[1:3, 0], dst.at[1, :, 1], base, (lat, lon_p, t))
        send(grid.at[0, 1:3], dst.at[2, 1], base + 1, (lat_p, lon, t))
        send(grid.at[3, 0], dst.at[3, 0, 1], base + 2, (lat, lon_p, t))
        send(grid.at[0, 3], dst.at[3, 1, 0], base + 3, (lat_p, lon, t))
        send(grid.at[0, 0], dst.at[3, 1, 1], base + 4, (lat_p, lon_p, t))

    def halo_parts(dst):
        return [dst.at[1, :, 1], dst.at[2, 1], dst.at[3, 0, 1], dst.at[3, 1, 0], dst.at[3, 1, 1]]

    side = t // 2
    is_mid = (t == 1) | (t == 2)
    is_edge = jnp.logical_not(is_mid)
    partner = 2 * side + 1 - t % 2
    far_mid = 2 - side
    far_edge = 3 - 3 * side
    far_slot = jnp.where(is_mid, 1, 2)

    def on_line(where):
        return (lat, lon, where)

    def spread_start(name, n, src, dst, i):
        base = SLOTS[name] + i
        send(src, dst, base + n * far_slot, on_line(far_mid), base + n)

        @pl.when(is_mid)
        def _():
            send(src, dst, base + n, on_line(far_edge), base + 2 * n)

        send(src, dst, base, on_line(partner), base)

    def spread_relay(name, n, buf, i):
        base = SLOTS[name] + i

        @pl.when(is_mid)
        def _():
            chunk = buf.at[far_edge, i]
            got(chunk, base + 2 * n)
            send(chunk, chunk, base + 2 * n, on_line(partner), base + 3 * n)

    def spread_wait(name, n, buf, i):
        base = SLOTS[name] + i
        got(buf.at[partner, i], base)
        got(buf.at[far_mid, i], base + n)

        @pl.when(is_edge)
        def _():
            got(buf.at[far_edge, i], base + 2 * n)

    def spread_drain(name, n, chunk, i):
        base = SLOTS[name] + i
        sent(chunk, base)
        sent(chunk, base + n)

        @pl.when(is_mid)
        def _():
            sent(chunk, base + 2 * n)
            sent(chunk, base + 3 * n)

    def sum_start(name, part, recv, relay, g):
        base = SLOTS[name] + g

        @pl.when(is_edge)
        def _():
            send(part.at[far_edge, g], relay.at[g], base + 6, on_line(partner), base + 4)

        send(part.at[far_mid, g], recv.at[t, g], base + 2 * far_slot, on_line(far_mid), base + 2)
        send(part.at[partner, g], recv.at[t, g], base, on_line(partner), base)

    def sum_relay(name, part, recv, relay, g):
        base = SLOTS[name] + g

        @pl.when(is_mid)
        def _():
            got(relay.at[g], base + 6)
            part[far_edge, g] = (part[far_edge, g].astype(F32) + relay[g].astype(F32)).astype(BF)
            send(part.at[far_edge, g], recv.at[t, g], base + 2, on_line(far_edge), base + 4)

    def sum_end(name, part, recv, g):
        base = SLOTS[name] + g
        got(recv.at[partner, g], base)
        got(recv.at[far_mid, g], base + 2)

        @pl.when(is_mid)
        def _():
            got(recv.at[far_edge, g], base + 4)

        @pl.when(is_edge)
        def _():
            recv[far_edge, g] = jnp.zeros(recv.shape[2:], BF)

        total = part[t, g].astype(F32)
        for src in (partner, far_mid, far_edge):
            total = total + recv[src, g].astype(F32)
        return total

    def give_fields(w, src):
        spread_start("fields", 4, src, x_own.at[w], w)

    halo(fields, x_own, SLOTS["halo_f"])

    piece_rows = pl.ds(pl.multiple_of(lx * 48, 16), 48)
    has_piece = ly < 3

    def piece(y, x):
        rows = pl.ds(pl.multiple_of(x * 48, 16), 48)
        return wcol.at[1:4, rows, pl.ds(pl.multiple_of(y * 128, 128), 128)]

    @pl.when(has_piece)
    def _():
        for d in (1, 2, 3):
            cols = pl.ds(pl.multiple_of(ring(t, d, 4) * SH + ly * 128, 128), 128)
            here = pl.ds(pl.multiple_of(ly * 128, 128), 128)
            send(wout.at[piece_rows, cols], wcol.at[d, piece_rows, here], SLOTS["wcol_z"] + d - 1, tp_dev(d))

    give_fields(0, fields.at[1:3, 1:3])
    cut_blocks(cot_grid, cot)
    keep_grid(cot, cbuf)
    keep(wout.at[:, pl.ds(pl.multiple_of(t * SH, 128), SH)], wcol.at[0])

    def place(n):
        a, b, c, d = (n >> 5) & 1, (n >> 4) & 1, (n >> 2) & 3, n & 3
        return 4 * a + c, 4 * b + d

    def iota(shape, dim):
        return lax.broadcasted_iota(jnp.int32, shape, dim)

    def hot(flag):
        return jnp.where(flag, 1.0, 0.0)

    row_of, col_of = place(iota((CELLS, CELLS), 0))
    order = hot(iota((CELLS, CELLS), 1) == row_of * WIN + col_of).astype(BF)
    swapped = nn(order, index[...].astype(F32).astype(BF)).astype(BF)
    idx = nt(swapped, order)
    for c in range(NPAIR // 128):
        idx_row[0:1, c * 128:(c + 1) * 128] = jnp.concatenate([idx[2 * c:2 * c + 1], idx[2 * c + 1:2 * c + 2]], axis=1)

    cell = iota((NWIN * CELLS, 16), 0)
    row_of, col_of = place(cell)
    row_of, col_of = row_of + WIN * (cell >> 7), col_of + WIN * ((cell >> 6) & 1)
    picked_rows = nn(hot(iota((NWIN * CELLS, 16), 1) == row_of).astype(BF), mask[...].astype(F32).astype(BF))
    labels = jnp.sum(hot(iota((NWIN * CELLS, 16), 1) == col_of) * picked_rows, axis=1, keepdims=True)
    lab_col[...] = labels + 4.0 * (iota((NWIN * CELLS, 1), 0) >> 6).astype(F32)

    own[1].wait()
    got(halo_parts(x_own)[0], SLOTS["halo_f"])
    give_fields(1, x_own.at[1])
    own[2].wait()
    got(halo_parts(x_own)[1], SLOTS["halo_f"] + 1)
    give_fields(2, x_own.at[2])
    own[3].wait()
    for part in (2, 3, 4):
        got(halo_parts(x_own)[part], SLOTS["halo_f"] + part)
    give_fields(3, x_own.at[3])

    @pl.when(has_piece)
    def _():
        for d in (1, 2, 3):
            here = pl.ds(pl.multiple_of(ly * 128, 128), 128)
            got(wcol.at[d, piece_rows, here], SLOTS["wcol_z"] + d - 1)
        for o in range(15):
            send(piece(ly, lx), piece(ly, lx), SLOTS["wcol_p"] + o, plane_dev(o))

    halo(cot, cbuf, SLOTS["halo_c"])

    tab_pad[...] = jnp.zeros_like(tab_pad)
    tab_pad[0:HEADS, 0:table.shape[1]] = table[...]
    tab = jnp.concatenate([*split3(tab_pad[...]), jnp.zeros((8, TABLE), F32)], axis=0).astype(BF)
    entry = iota((TABLE, 512), 0).astype(F32)
    for c in range(NPAIR // 512):
        span = slice(c * 512, (c + 1) * 512)
        picked = hot(entry == idx_row[0:1, span]).astype(BF)
        onehot[:, span] = picked
        parts = nn(tab, picked)
        bias = parts[0:8] + parts[8:16] + parts[16:24]
        sig = 1.0 / (1.0 + jnp.exp(-bias))
        bsrow[:, span] = sig
        for k in range(8):
            for h in range(HEADS):
                at = 8 * c + k
                pair = jnp.concatenate([16.0 * sig[h:h + 1, k * CELLS:(k + 1) * CELLS]] * 2, axis=1)
                bsig[h, at:at + 1, :] = pair
                bsig[h, CELLS + at:CELLS + at + 1, :] = pair
    tacc[...] = jnp.zeros_like(tacc)
    sacc[...] = jnp.zeros_like(sacc)
    gacc[...] = jnp.zeros_like(gacc)
    scales = jnp.exp(logs[...])

    own[0].wait()

    eye = iota((2 * CELLS, 2 * CELLS), 0) == iota((2 * CELLS, 2 * CELLS), 1)

    def forward(g):
        for w in (2 * g, 2 * g + 1):
            spread_relay("fields", 4, xbuf, w)
        for w in (2 * g, 2 * g + 1):
            spread_wait("fields", 4, xbuf, w)
        proj = jnp.zeros((2 * CELLS, 3 * AW), F32)
        for src in range(4):
            proj = proj + nt(xbuf[src, 2 * g:2 * g + 2].reshape(2 * CELLS, SH), wt[:, src * SH:(src + 1) * SH])
        column = lab_col[2 * g * CELLS:2 * (g + 1) * CELLS]
        row = jnp.sum(jnp.where(eye, column, 0.0), axis=0, keepdims=True)
        same = row == column
        heads = range(HEADS)

        def slot(kind, h):
            at = kind * AW + h * HD
            return proj[:, at:at + HD]

        q = [slot(0, h) for h in heads]
        k = [slot(1, h) for h in heads]
        v = [slot(2, h).astype(BF) for h in heads]
        rq = [lax.rsqrt(jnp.sum(q[h] * q[h], axis=1, keepdims=True) + 1e-06) for h in heads]
        rk = [lax.rsqrt(jnp.sum(k[h] * k[h], axis=1, keepdims=True) + 1e-06) for h in heads]
        q_hat = [(q[h] * rq[h]).astype(BF) for h in heads]
        k_hat = [(k[h] * rk[h]).astype(BF) for h in heads]
        cosine = [nt(q_hat[h], k_hat[h]) for h in heads]
        power = [scales[:, h:h + 1] * (cosine[h] - 1.0) + (bsig[h] - 16.0) for h in heads]
        weight = [jnp.where(same, jnp.exp(power[h]), 0.0) for h in heads]
        total = [jnp.sum(weight[h], axis=1, keepdims=True) for h in heads]
        prob = [(weight[h] * (1.0 / total[h])).astype(BF) for h in heads]
        attended = [nn(prob[h], v[h]).astype(BF) for h in heads]
        for i in (0, 1):
            for h in heads:
                at = i * AW + h * HD
                abuf[t, g, :, at:at + HD] = attended[h][i * CELLS:(i + 1) * CELLS]
        for h in heads:
            qs[g, h] = q_hat[h]
            ks[g, h] = k_hat[h]
            vs[g, h] = v[h]
            probs[g, h] = prob[h]
            coss[g, h] = cosine[h]
            rqs[g, h] = rq[h]
            rks[g, h] = rk[h]
        spread_start("att", 2, abuf.at[t, g], abuf.at[t, g], g)

    gain = gain_ref[...].reshape(1, SH)
    shift = shift_ref[...].reshape(1, SH)
    lane = iota((2 * CELLS, 128), 1)

    def unpack(pair):
        return jnp.concatenate([pair[:, :AW], pair[:, AW:]], axis=0)

    def cells_of(buf, g):
        return buf[2 * g:2 * g + 2].reshape(2 * CELLS, SH).astype(F32)

    def mix(g):
        spread_relay("att", 2, abuf, g)
        spread_wait("att", 2, abuf, g)
        total = jnp.zeros((2 * CELLS, SH), F32)
        for d in range(4):
            total = total + nn(unpack(abuf[ring(t, -d, 4), g]), wcol[d])
        mixed[g] = total
        grad_norm = cells_of(cbuf, g) * gain
        packed = jnp.zeros((2 * CELLS, 128), F32)
        for i, v in enumerate((total, total * total, grad_norm, grad_norm * total)):
            packed = jnp.where(lane == i, jnp.sum(v, axis=1, keepdims=True), packed)
        stat_all[t, g] = jnp.transpose(packed)[0:8]
        mine = stat_all.at[t, g]
        for d in (1, 2, 3):
            send(mine, mine, SLOTS["stat"] + (d - 1) * 2 + g, tp_dev(d))

    def normalise(g):
        for d in (1, 2, 3):
            got(stat_all.at[ring(t, -d, 4), g], SLOTS["stat"] + (d - 1) * 2 + g)
        totals = stat_all[0, g] + stat_all[1, g] + stat_all[2, g] + stat_all[3, g]
        packed = jnp.transpose(jnp.concatenate([totals, jnp.zeros((120, 128), F32)], axis=0))
        mean = packed[:, 0:1] / CH
        variance = packed[:, 1:2] / CH - mean * mean
        inv_std = 1.0 / jnp.sqrt(variance + 1e-05)
        grad_mean = packed[:, 2:3] / CH
        cross_mean = inv_std * (packed[:, 3:4] - mean * packed[:, 2:3]) / CH
        normed = (mixed[g] - mean) * inv_std
        rows = cells_of(cbuf, g)
        grad = (inv_std * (rows * gain - grad_mean - normed * cross_mean)).astype(BF)
        gmix[g] = grad
        for d in (2, 1, 3, 0):
            dst = ring(t, d, 4)
            part = nt(grad, wcol[(4 - d) % 4])
            ga_send[dst, g] = jnp.concatenate([part[:CELLS], part[CELLS:]], axis=1).astype(BF)
        sum_start("gatt", ga_send, ga_recv, ga_relay, g)
        base = xbuf[t, 2 * g:2 * g + 2].reshape(2 * CELLS, SH).astype(F32)
        obuf[2 * g:2 * g + 2] = (base + (gain * normed + shift)).astype(BF).reshape(2, 2, 2, 16, SH)
        gacc[0:1, :] += jnp.sum(rows * normed, axis=0, keepdims=True)
        gacc[1:2, :] += jnp.sum(rows, axis=0, keepdims=True)

    def backward(g):
        total = sum_end("gatt", ga_send, ga_recv, g)
        grad_att = unpack(total.astype(BF))
        heads = range(HEADS)
        ga = [grad_att[:, h * HD:(h + 1) * HD] for h in heads]
        prob = [probs[g, h] for h in heads]
        q_hat = [qs[g, h] for h in heads]
        k_hat = [ks[g, h] for h in heads]
        grad_prob = [nt(ga[h], vs[g, h]) for h in heads]
        grads_v = [tn(prob[h], ga[h]) for h in heads]
        prob_f = [prob[h].astype(F32) for h in heads]
        inner = [jnp.sum(prob_f[h] * grad_prob[h], axis=1, keepdims=True) for h in heads]
        grad_logit = [prob_f[h] * (grad_prob[h] - inner[h]) for h in heads]
        grad_cos = [(grad_logit[h] * scales[:, h:h + 1]).astype(BF) for h in heads]
        gq = [nn(grad_cos[h], k_hat[h]) for h in heads]
        gk = [tn(grad_cos[h], q_hat[h]) for h in heads]
        for h in heads:
            tacc[h] += grad_logit[h]
            sacc[h] += grad_logit[h] * coss[g, h]
        q_float = [q_hat[h].astype(F32) for h in heads]
        k_float = [k_hat[h].astype(F32) for h in heads]
        q_in = [jnp.sum(q_float[h] * gq[h], axis=1, keepdims=True) for h in heads]
        k_in = [jnp.sum(k_float[h] * gk[h], axis=1, keepdims=True) for h in heads]
        grads_q = [(gq[h] - q_float[h] * q_in[h]) * rqs[g, h] for h in heads]
        grads_k = [(gk[h] - k_float[h] * k_in[h]) * rks[g, h] for h in heads]
        stacked = jnp.concatenate(grads_q + grads_k + grads_v, axis=1).astype(BF)
        for d in (2, 1, 3, 0):
            dst = ring(t, d, 4)
            gs_send[dst, g] = nn(stacked, wt[:, pl.ds(pl.multiple_of(dst * SH, 128), SH)]).astype(BF)
        sum_start("gsh", gs_send, gs_recv, gs_relay, g)

    def finish(g):
        total = sum_end("gsh", gs_send, gs_recv, g) + cells_of(cbuf, g)
        gobuf[2 * g:2 * g + 2] = total.astype(BF).reshape(2, 2, 2, 16, SH)

    def give_first(buf, out, base):
        out[1:3, 1:3] = buf[0]
        out[1:3, 3] = buf[1, :, 0]
        send(buf.at[1, :, 1], out.at[1:3, 0], base, (lat, lon_n, t))

    def give_second(buf, out, base):
        send(buf.at[2, 1], out.at[0, 1:3], base + 1, (lat_n, lon, t))
        send(buf.at[3, 0, 1], out.at[3, 0], base + 2, (lat, lon_n, t))
        send(buf.at[3, 1, 0], out.at[0, 3], base + 3, (lat_n, lon, t))
        send(buf.at[3, 1, 1], out.at[0, 0], base + 4, (lat_n, lon_n, t))
        out[3, 1:3] = buf[2, 0]
        out[3, 3] = buf[3, 0, 0]

    def back_parts(out):
        return [out.at[1:3, 0], out.at[0, 1:3], out.at[3, 0], out.at[0, 3], out.at[0, 0]]

    def weight_first():
        for group in range(4):
            wacc[group] = tn(unpack(abuf[group, 0]), gmix[0])

    def weight_start():
        for j in (0, 1):
            far = 2 * (1 - core) + j
            wc_send[j] = (wacc[far] + tn(unpack(abuf[far, 1]), gmix[1])).astype(BF)
        send(wc_send, wc_recv, SLOTS["w_core"], sib)
        for j in (0, 1):
            near = 2 * core + j
            wacc[near] = wacc[near] + tn(unpack(abuf[near, 1]), gmix[1])

    def rows_of(y, x):
        return pl.ds(pl.multiple_of(x * 48 + y * 16, 16), 16)

    def weight_plane():
        got(wc_recv, SLOTS["w_core"])
        for j in (0, 1):
            total = wacc[2 * core + j] + wc_recv[j].astype(F32)
            wacc[2 * core + j] = total
            wp_send[j] = total.astype(BF)
        for o in range(15):
            y, x = plane(o)

            @pl.when(y < 3)
            def _():
                send(wp_send.at[:, rows_of(y, x)], wp_recv.at[o], SLOTS["w_p"] + o, plane_dev(o))

    holder = t // 2 == core

    def weight_z():
        @pl.when(has_piece)
        def _():
            for o in range(15):
                got(wp_recv.at[o], SLOTS["w_p"] + o)
            for j in (0, 1):
                total = wacc[2 * core + j, rows_of(ly, lx), :]
                for o in range(15):
                    total = total + wp_recv[o, j].astype(F32)
                wp_sum[j] = total.astype(BF)
            for j in (0, 1):
                keeper = 2 * core + j
                for dz in range(4):
                    @pl.when((keeper != t) if dz == 0 else (keeper >= 0))
                    def _():
                        dev = (ring(zh, dz, 4) * 2 + core, lon, keeper)
                        send(wp_sum.at[j], bz.at[zh, t], SLOTS["w_z"] + zh * 4 + t, dev, SLOTS["w_zs"] + 4 * j + dz)

    def weight_back_plane():
        @pl.when(holder & has_piece)
        def _():
            bz[zh, t] = wp_sum[t % 2]
            for z in range(4):
                for src in range(4):
                    @pl.when((zh != z) | (t != src))
                    def _():
                        got(bz.at[z, src], SLOTS["w_z"] + z * 4 + src)

            for src in range(4):
                total = bz[0, src].astype(F32)
                for z in range(1, 4):
                    total = total + bz[z, src].astype(F32)
                out_w[rows_of(ly, lx), src * SH:(src + 1) * SH] = total.astype(BF)
            mine = out_w.at[rows_of(ly, lx)]
            for o in range(15):
                send(mine, mine, SLOTS["back_p"] + o, plane_dev(o))
            send(mine, mine, SLOTS["back_core"] + lx * 3 + ly, sib)

    def weight_back_core():
        @pl.when(holder)
        def _():
            for o in range(15):
                y, x = plane_from(o)

                @pl.when(y < 3)
                def _():
                    mine = out_w.at[rows_of(y, x)]
                    got(mine, SLOTS["back_p"] + o)
                    send(mine, mine, SLOTS["back_core"] + x * 3 + y, sib)

    def small_start():
        folded_t = [tacc[h, :CELLS, :CELLS] + tacc[h, CELLS:, CELLS:] for h in range(HEADS)]
        for c in range(NPAIR // 128):
            for h in range(HEADS):
                pair = [folded_t[h][2 * c + i:2 * c + i + 1, :] for i in (0, 1)]
                flat[h:h + 1, c * 128:(c + 1) * 128] = jnp.concatenate(pair, axis=1)
        spread = bsrow[0:HEADS, :]
        terms = flat[0:HEADS, :] * 16.0 * spread * (1.0 - spread)
        pad = jnp.zeros((8 - HEADS, NPAIR), F32)
        pieces = jnp.concatenate([v for p in split3(terms) for v in (p, pad)], axis=0).astype(BF)
        folded = nt(pieces, onehot[...])
        sm_p[lon] = folded[0:8] + folded[8:16] + folded[16:24]
        for h in range(HEADS):
            amount = jnp.sum(jnp.sum(sacc[h], axis=1, keepdims=True), axis=0, keepdims=True) * scales[:, h:h + 1]
            sm_p[lon, h:h + 1, TABLE - 1:TABLE] = amount
        sm_p[lon, 3:5, :] = gacc[0:2, 0:TABLE]
        sm_p[lon, 5:6, :] = jnp.concatenate([gacc[0:1, TABLE:SH], gacc[1:2, TABLE:SH]], axis=1)
        for o in range(15):
            send(sm_p.at[lon], sm_p.at[lon], SLOTS["s_p"] + o, plane_dev(o))

    def small_lat():
        for o in range(15):
            y, x = plane_from(o)
            got(sm_p.at[y * 4 + x], SLOTS["s_p"] + o)
        total = sm_p[0]
        for i in range(1, 16):
            total = total + sm_p[i]
        sm_l[lat] = total
        for d in range(1, 8):
            send(sm_l.at[lat], sm_l.at[lat], SLOTS["s_l"] + d - 1, (ring(lat, d, 8), lon, t))

    def small_end():
        for d in range(1, 8):
            got(sm_l.at[ring(lat, -d, 8)], SLOTS["s_l"] + d - 1)
        total = sm_l[0]
        for i in range(1, 8):
            total = total + sm_l[i]
        out_s[...] = jnp.zeros_like(out_s)
        out_s[0:2, 0:TABLE] = total[3:5]
        out_s[0:1, TABLE:SH] = total[5:6, 0:128]
        out_s[1:2, TABLE:SH] = total[5:6, 128:256]
        out_s[2:5, 0:TABLE] = total[0:3]

    forward(0)
    forward(1)
    own[8].wait()
    for o in range(15):
        y, x = plane_from(o)

        @pl.when(y < 3)
        def _():
            got(piece(y, x), SLOTS["wcol_p"] + o)

    for i in (4, 5, 6, 7):
        own[i].wait()
    for i in range(5):
        got(halo_parts(cbuf)[i], SLOTS["halo_c"] + i)
    mix(0)
    normalise(0)
    mix(1)
    sum_relay("gatt", ga_send, ga_recv, ga_relay, 0)
    weight_first()
    normalise(1)
    weight_start()
    sum_relay("gatt", ga_send, ga_recv, ga_relay, 1)
    give_first(obuf, out_f, SLOTS["out_f"])
    give_second(obuf, out_f, SLOTS["out_f"])
    backward(0)
    weight_plane()
    backward(1)
    sum_relay("gsh", gs_send, gs_recv, gs_relay, 0)
    small_start()
    sum_relay("gsh", gs_send, gs_recv, gs_relay, 1)
    weight_z()
    finish(0)
    give_first(gobuf, out_g, SLOTS["out_g"])
    small_lat()
    weight_back_plane()
    finish(1)
    give_second(gobuf, out_g, SLOTS["out_g"])
    weight_back_core()
    small_end()

    for i in range(5):
        got(back_parts(out_f)[i], SLOTS["out_f"] + i)
        got(back_parts(out_g)[i], SLOTS["out_g"] + i)

    for base, parts in (("halo_f", halo_parts(x_own)), ("halo_c", halo_parts(cbuf)),
                        ("out_f", back_parts(out_f)), ("out_g", back_parts(out_g))):
        for i in range(5):
            sent(parts[i], SLOTS[base] + i)

    for w in range(NWIN):
        spread_drain("fields", 4, xbuf.at[0, 0], w)
    for g in range(GROUPS):
        spread_drain("att", 2, abuf.at[0, 0], g)
        for i in range(3):
            sent(stat_all.at[0, 0], SLOTS["stat"] + 2 * i + g)
            sent(ga_send.at[0, 0], SLOTS["gatt"] + 2 * i + g)
            sent(gs_send.at[0, 0], SLOTS["gsh"] + 2 * i + g)

    @pl.when(has_piece)
    def _():
        for d in range(3):
            sent(wcol.at[0, 0:48, 0:128], SLOTS["wcol_z"] + d)
            for j in (0, 1):
                sent(wp_sum.at[j], SLOTS["w_zs"] + 4 * j + d + 1)
        for o in range(15):
            sent(wcol.at[1:4, 0:48, 0:128], SLOTS["wcol_p"] + o)

        for j in (0, 1):
            @pl.when(2 * core + j != t)
            def _():
                sent(wp_sum.at[j], SLOTS["w_zs"] + 4 * j)

    @pl.when(holder & has_piece)
    def _():
        for o in range(15):
            sent(out_w.at[0:16], SLOTS["back_p"] + o)
        sent(out_w.at[0:16], SLOTS["back_core"] + lx * 3 + ly)

    for o in range(15):
        sent(sm_p.at[0], SLOTS["s_p"] + o)

        @pl.when(plane(o)[0] < 3)
        def _():
            sent(wp_send.at[:, 0:16], SLOTS["w_p"] + o)

        @pl.when(holder & (plane_from(o)[0] < 3))
        def _():
            y, x = plane_from(o)
            sent(out_w.at[0:16], SLOTS["back_core"] + x * 3 + y)

    for d in range(7):
        sent(sm_l.at[0], SLOTS["s_l"] + d)
    sent(wc_send, SLOTS["w_core"])

    @pl.when(jnp.logical_not(holder))
    def _():
        for x in range(4):
            for y in range(3):
                got(out_w.at[x * 48 + y * 16:x * 48 + y * 16 + 16], SLOTS["back_core"] + x * 3 + y)


def per_device(
    fields, w_qkv, w_out, log_scale, bias_table, bias_index, mask_ids, norm_gain, norm_shift, cotangent
):
    rows = bias_table.shape[0]
    wt = w_qkv.transpose(1, 2, 0).reshape(3 * AW, CH)
    hbm = pl.BlockSpec(memory_space=pltpu.HBM)
    vmem = pl.BlockSpec(memory_space=pltpu.VMEM)
    scratch = [
        ((4, 4, 16, SH), BF), ((4, 4, 16, SH), BF), ((4, 4, 2, 2, 16, SH), BF), ((4, 2, 2, 16, SH), BF), ((4, AW, SH), BF),
        ((4, 2, CELLS, SH), BF), ((TABLE, NPAIR), BF), ((8, NPAIR), F32), ((8, NPAIR), F32), ((8, TABLE), F32),
        ((HEADS, 2 * CELLS, 2 * CELLS), F32), ((NWIN * CELLS, 1), F32),
        ((2, HEADS, 2 * CELLS, HD), BF), ((2, HEADS, 2 * CELLS, HD), BF), ((2, HEADS, 2 * CELLS, HD), BF),
        ((2, HEADS, 2 * CELLS, 2 * CELLS), BF), ((2, HEADS, 2 * CELLS, 2 * CELLS), F32),
        ((2, HEADS, 2 * CELLS, 1), F32), ((2, HEADS, 2 * CELLS, 1), F32),
        ((2, 2 * CELLS, SH), F32), ((4, 2, 8, 128), F32), ((2, 2 * CELLS, SH), BF),
        ((4, 2, CELLS, SH), BF), ((4, 2, CELLS, SH), BF), ((2, CELLS, SH), BF),
        ((4, 2, 2 * CELLS, SH), BF), ((4, 2, 2 * CELLS, SH), BF), ((2, 2 * CELLS, SH), BF),
        ((4, 2, 2, 16, SH), BF), ((4, 2, 2, 16, SH), BF),
        ((HEADS, 2 * CELLS, 2 * CELLS), F32), ((HEADS, 2 * CELLS, 2 * CELLS), F32), ((8, SH), F32), ((8, NPAIR), F32),
        ((2, AW, SH), BF), ((2, AW, SH), BF), ((4, AW, SH), F32),
        ((2, AW, SH), BF), ((15, 2, 16, SH), BF), ((2, 16, SH), BF), ((4, 4, 16, SH), BF),
        ((16, 8, TABLE), F32), ((8, 8, TABLE), F32),
    ]
    out_f, out_g, out_w, out_s = pl.pallas_call(
        whole_kernel,
        out_shape=(
            jax.ShapeDtypeStruct((4, 4, 16, SH), BF),
            jax.ShapeDtypeStruct((4, 4, 16, SH), BF),
            jax.ShapeDtypeStruct((AW, CH), BF),
            jax.ShapeDtypeStruct((8, SH), F32),
        ),
        in_specs=[vmem, vmem, vmem, hbm, vmem, vmem, vmem, vmem, vmem, vmem],
        out_specs=(vmem, vmem, vmem, vmem),
        scratch_shapes=[pltpu.VMEM(shape, kind) for shape, kind in scratch] + [
            pltpu.SemaphoreType.DMA((9,)),
            pltpu.SemaphoreType.DMA((COUNT,)),
            pltpu.SemaphoreType.DMA((COUNT,)),
        ],
        compiler_params=pltpu.CompilerParams(
            collective_id=0, has_side_effects=True, vmem_limit_bytes=40 * 1024 * 1024
        ),
        cost_estimate=pl.CostEstimate(flops=2_000_000_000, bytes_accessed=5_000_000, transcendentals=200_000),
    )(
        fields, cotangent, wt, w_out, log_scale.reshape(1, HEADS), bias_table.T, bias_index, mask_ids,
        norm_gain, norm_shift,
    )
    shapes = (
        (fields.shape, BF), (fields.shape, BF), ((AW, CH), BF), ((HEADS, rows), F32), ((HEADS,), F32),
        ((SH,), F32), ((SH,), F32),
    )
    block_out, grad_fields, grad_w_out, grad_table, grad_scale, grad_gain, grad_shift = pl.pallas_call(
        write_kernel,
        out_shape=tuple(jax.ShapeDtypeStruct(shape, kind) for shape, kind in shapes),
        in_specs=[vmem] * 4,
        out_specs=(vmem,) * 7,
        compiler_params=pltpu.CompilerParams(vmem_limit_bytes=16 * 1024 * 1024),
        cost_estimate=pl.CostEstimate(flops=1_000_000, bytes_accessed=2_000_000, transcendentals=0),
    )(out_f, out_g, out_w, out_s)
    return (block_out, grad_fields, grad_w_out, grad_table.T, grad_scale, grad_gain, grad_shift)


def solution(mesh):
    in_specs = (
        P("lat", "lon", "tp"), P(None, None, "tp"), P("tp", None), P("tp"), P(None, "tp"), P(),
        P("lat", "lon"), P("tp"), P("tp"), P("lat", "lon", "tp"),
    )
    out_specs = (
        P("lat", "lon", "tp"), P("lat", "lon", "tp"), P("tp", None), P(None, "tp"), P("tp"), P("tp"), P("tp"),
    )
    return jax.shard_map(per_device, mesh=mesh, in_specs=in_specs, out_specs=out_specs, check_vma=False)
```

time: 1050 us -> 109 us (0.10)
  blocking collectives: 804 us -> 0 us
  waiting for transfers between devices: 122 us -> 0 us
  Pallas kernels: 0 us -> 99.1 us
  starting transfers between devices: 57.2 us -> 0 us
  other arithmetic: 17.7 us -> 0 us
  matrix products: 17.6 us -> 0 us
  between operations: 14.9 us -> 0.66 us
    psum x2 -> x0, blocking collectives: 771 us -> none  [the longest x1 762 us: per_device(): grad_w_out = lax.psum(weight_cols, ('lat', 'lon')).astype(jnp.bfloat16)]
    pallas_call x0 -> x2, Pallas kernels: none -> 99.1 us  [the longest x1 98 us: per_device(): pl.pallas_call(whole_kernel, out_shape=(jax.ShapeDtypeStruct((4, 4, 16, S...]
    ppermute x8 -> x0, waiting for transfers between devices: 59.4 us -> none  [shifted_2(): lax.ppermute(value, axis, [(i, (i + by) % count) for i in range(count)])]
    ppermute x8 -> x0, starting transfers between devices: 57.1 us -> none  [shifted_2(): lax.ppermute(value, axis, [(i, (i + by) % count) for i in range(count)])]
    psum x1 -> x0, waiting for transfers between devices: 48 us -> none  [per_device(): whole = lax.psum(head_terms.astype(jnp.bfloat16), 'tp').astype(jnp.float32)]
    all_gather x2 -> x0, blocking collectives: 32.9 us -> none  [the longest x1 17.6 us: per_device(): piece = lax.all_gather(shifted, 'tp', axis=2, tiled=True)]
    dot_general x13 -> x0, matrix products: 17.6 us -> none  [the longest x6 5.78 us: mult(): return jnp.einsum(spec, left, right, preferred_element_type=jnp.float32)]
    unnamed x3 -> x0, waiting for transfers between devices: 14.1 us -> none
  transfers between devices with their start and end apart: 10 -> 0, of which waited for: 6 -> 0; matrix products, arithmetic and copies ran while one was open for 2% -> 0% of each run, Pallas kernels for 0% -> 0%
where the time goes in v1:
time: 109 us; the launch traced here: 108 us
  Pallas kernels  99.1 us (91%)
  local copies, waits for them, and re-layouts  8.54 us (8%)
    pallas_call x1, Pallas kernels, per_device(): pl.pallas_call(whole_kernel, out_shape=(jax.ShapeDtypeStruct((4, 4, 16, S...  98 us
    unnamed x20, local copies, waits for them, and re-layouts  8.54 us

profile of v1, /device:TPU:1, one launch (start us, length us, event | category | flops | bytes accessed | tf_op | source)
XLA Modules:
  0.0 108.3 jit_solution(1186955874349406172)
XLA Ops:
  0.6 0.0 copy-start
  0.6 1.5 %copy-done = bf16[1536,3,192]{0,2,1:T(8,128)(2,1)S(1)} copy-done((bf16[1536,3,192]{0,2,1:T(8,128)(2,1)S(1)}, bf16[1536,3,192]{0,2,1:T(8,128)(2,1)}, u32[]{:S(2)}) %copy-start) | copy-done | bytes 1769496
  2.1 0.0 copy-start.1
  2.1 1.1 copy-done.1
  3.2 0.0 copy-start.2
  3.2 0.9 copy-done.2
  4.1 0.0 copy-start.3
  4.1 0.9 copy-done.3
  5.0 0.0 copy-start.4
  5.0 0.8 copy-done.4
  5.8 0.0 copy-start.5
  5.8 0.7 copy-done.5
  6.5 0.0 copy-start.6
  6.5 0.7 copy-done.6
  7.2 0.0 copy-start.7
  7.2 0.7 copy-done.7
  7.9 0.0 copy-start.8
  7.9 0.7 copy-done.8
  8.5 0.0 copy-start.9
  8.5 0.7 copy-done.9
  9.2 98.0 %shard_map.153 = (bf16[4,4,16,384]{3,2,1,0:T(8,128)(2,1)S(1)}, bf16[4,4,16,384]{3,2,1,0:T(8,128)(2,1)S(1)}, bf16[192,1536]{1,0:T(8,128)(2,1)S(1)}, f32[8,384]{1,0:T(8,128)S(1)}) custom-call(bf16[16,16,384]{2,1,0:T(8,128)(2,1)S(1)} %copy-done.2, bf16[16,16,384]{2,1,0:T(8,128)(2,1)S(1)} %copy-done.3, bf16[576,1536]{1,0:T(8,128)(2,1)S(1)} %bitcast.6, ...), custom_call_target="tpu_custom_call" | custom-call | flops 2000000000 | bytes 5000000 | tf_op jit(solution)/shard_map/pallas_call | solution.py:761
  107.2 1.1 shard_map.154
Async XLA Ops:
  0.6 1.5 %copy-start = (bf16[1536,3,192]{0,2,1:T(8,128)(2,1)S(1)}, bf16[1536,3,192]{0,2,1:T(8,128)(2,1)}, u32[]{:S(2)}) copy-start(bf16[1536,3,192]{0,2,1:T(8,128)(2,1)} %param.11) | copy-start | bytes 5308420
  2.1 1.1 copy-start.1
  3.2 0.9 copy-start.2
  4.1 0.9 copy-start.3
  5.0 0.8 copy-start.4
  5.8 0.7 copy-start.5
  6.5 0.7 copy-start.6
  7.2 0.7 copy-start.7
  7.9 0.7 copy-start.8
  8.5 0.7 copy-start.9

commit v2 on v1

--- a/solution.py
+++ b/solution.py
@@ -96,9 +96,9 @@
 
 
 def whole_kernel(
-    fields_grid, cot_grid, wt, wout, logs, table, index, mask, gain_ref, shift_ref,
+    fields_hbm, cot_hbm, wt_hbm, wout, logs, table, index, mask, gain_ref, shift_ref,
     out_f, out_g, out_w, out_s,
-    fields, cot, xbuf, cbuf, wcol, abuf, onehot, bsrow, idx_row, tab_pad, bsig, lab_col, qs, ks, vs, probs, coss, rqs, rks,
+    fields_grid, cot_grid, wt, fields, cot, xbuf, cbuf, wcol, abuf, onehot, bsrow, idx_row, tab_pad, bsig, lab_col, qs, ks, vs, probs, coss, rqs, rks,
     mixed, stat_all, gmix, ga_send, ga_recv, ga_relay, gs_send, gs_recv, gs_relay, obuf, gobuf, tacc, sacc, gacc, flat,
     wc_send, wc_recv, wacc, wp_send, wp_recv, wp_sum, bz, sm_p, sm_l, local_sem, ssem, rsem,
 ):
@@ -148,6 +148,16 @@
     def sent(src, slot):
         copy(src, src, slot, sib).wait_send()
 
+    own = []
+
+    def keep(src, dst):
+        own.append(pltpu.make_async_copy(src, dst, local_sem.at[len(own)]))
+        own[-1].start()
+
+    keep(fields_hbm, fields_grid)
+    keep(cot_hbm, cot_grid)
+    keep(wt_hbm, wt)
+
     partners = [plane_dev(o) for o in range(15)] + [(ring(lat, d, 8), lon, t) for d in range(1, 8)]
     partners += [(lat_p, lon_p, t), (lat_n, lon_n, t)] + [tp_dev(d) for d in (1, 2, 3)]
     partners += [(ring(zh, dz, 4) * 2 + core, lon, ring(t, dt, 4)) for dz in (1, 2, 3) for dt in (1, 2, 3)]
@@ -155,12 +165,6 @@
     for dev in partners:
         pl.semaphore_signal(barrier, inc=1, device_id=dev, device_id_type=MESH)
 
-    own = []
-
-    def keep(src, dst):
-        own.append(pltpu.make_async_copy(src, dst, local_sem.at[len(own)]))
-        own[-1].start()
-
     def keep_grid(grid, dst):
         keep(grid.at[1:3, 1:3], dst.at[0])
         keep(grid.at[1:3, 3], dst.at[1, :, 0])
@@ -168,6 +172,7 @@
         keep(grid.at[3, 3], dst.at[3, 0, 0])
 
     x_own = xbuf.at[t]
+    own[0].wait()
     cut_blocks(fields_grid, fields)
     keep_grid(fields, x_own)
 
@@ -289,6 +294,7 @@
             send(wout.at[piece_rows, cols], wcol.at[d, piece_rows, here], SLOTS["wcol_z"] + d - 1, tp_dev(d))
 
     give_fields(0, fields.at[1:3, 1:3])
+    own[1].wait()
     cut_blocks(cot_grid, cot)
     keep_grid(cot, cbuf)
     keep(wout.at[:, pl.ds(pl.multiple_of(t * SH, 128), SH)], wcol.at[0])
@@ -317,13 +323,13 @@
     labels = jnp.sum(hot(iota((NWIN * CELLS, 16), 1) == col_of) * picked_rows, axis=1, keepdims=True)
     lab_col[...] = labels + 4.0 * (iota((NWIN * CELLS, 1), 0) >> 6).astype(F32)
 
-    own[1].wait()
+    own[4].wait()
     got(halo_parts(x_own)[0], SLOTS["halo_f"])
     give_fields(1, x_own.at[1])
-    own[2].wait()
+    own[5].wait()
     got(halo_parts(x_own)[1], SLOTS["halo_f"] + 1)
     give_fields(2, x_own.at[2])
-    own[3].wait()
+    own[6].wait()
     for part in (2, 3, 4):
         got(halo_parts(x_own)[part], SLOTS["halo_f"] + part)
     give_fields(3, x_own.at[3])
@@ -361,7 +367,8 @@
     gacc[...] = jnp.zeros_like(gacc)
     scales = jnp.exp(logs[...])
 
-    own[0].wait()
+    own[2].wait()
+    own[3].wait()
 
     eye = iota((2 * CELLS, 2 * CELLS), 0) == iota((2 * CELLS, 2 * CELLS), 1)
 
@@ -636,7 +643,7 @@
 
     forward(0)
     forward(1)
-    own[8].wait()
+    own[11].wait()
     for o in range(15):
         y, x = plane_from(o)
 
@@ -644,7 +651,7 @@
         def _():
             got(piece(y, x), SLOTS["wcol_p"] + o)
 
-    for i in (4, 5, 6, 7):
+    for i in (7, 8, 9, 10):
         own[i].wait()
     for i in range(5):
         got(halo_parts(cbuf)[i], SLOTS["halo_c"] + i)
@@ -743,7 +750,7 @@
     hbm = pl.BlockSpec(memory_space=pltpu.HBM)
     vmem = pl.BlockSpec(memory_space=pltpu.VMEM)
     scratch = [
-        ((4, 4, 16, SH), BF), ((4, 4, 16, SH), BF), ((4, 4, 2, 2, 16, SH), BF), ((4, 2, 2, 16, SH), BF), ((4, AW, SH), BF),
+        ((16, 16, SH), BF), ((16, 16, SH), BF), ((576, CH), BF), ((4, 4, 16, SH), BF), ((4, 4, 16, SH), BF), ((4, 4, 2, 2, 16, SH), BF), ((4, 2, 2, 16, SH), BF), ((4, AW, SH), BF),
         ((4, 2, CELLS, SH), BF), ((TABLE, NPAIR), BF), ((8, NPAIR), F32), ((8, NPAIR), F32), ((8, TABLE), F32),
         ((HEADS, 2 * CELLS, 2 * CELLS), F32), ((NWIN * CELLS, 1), F32),
         ((2, HEADS, 2 * CELLS, HD), BF), ((2, HEADS, 2 * CELLS, HD), BF), ((2, HEADS, 2 * CELLS, HD), BF),
@@ -766,15 +773,15 @@
             jax.ShapeDtypeStruct((AW, CH), BF),
             jax.ShapeDtypeStruct((8, SH), F32),
         ),
-        in_specs=[vmem, vmem, vmem, hbm, vmem, vmem, vmem, vmem, vmem, vmem],
+        in_specs=[hbm, hbm, hbm, hbm, vmem, vmem, vmem, vmem, vmem, vmem],
         out_specs=(vmem, vmem, vmem, vmem),
         scratch_shapes=[pltpu.VMEM(shape, kind) for shape, kind in scratch] + [
-            pltpu.SemaphoreType.DMA((9,)),
+            pltpu.SemaphoreType.DMA((12,)),
             pltpu.SemaphoreType.DMA((COUNT,)),
             pltpu.SemaphoreType.DMA((COUNT,)),
         ],
         compiler_params=pltpu.CompilerParams(
-            collective_id=0, has_side_effects=True, vmem_limit_bytes=40 * 1024 * 1024
+            collective_id=0, has_side_effects=True, vmem_limit_bytes=60 * 1024 * 1024
         ),
         cost_estimate=pl.CostEstimate(flops=2_000_000_000, bytes_accessed=5_000_000, transcendentals=200_000),
     )(
@@ -790,7 +797,7 @@
         out_shape=tuple(jax.ShapeDtypeStruct(shape, kind) for shape, kind in shapes),
         in_specs=[vmem] * 4,
         out_specs=(vmem,) * 7,
-        compiler_params=pltpu.CompilerParams(vmem_limit_bytes=16 * 1024 * 1024),
+        compiler_params=pltpu.CompilerParams(vmem_limit_bytes=60 * 1024 * 1024),
         cost_estimate=pl.CostEstimate(flops=1_000_000, bytes_accessed=2_000_000, transcendentals=0),
     )(out_f, out_g, out_w, out_s)
     return (block_out, grad_fields, grad_w_out, grad_table.T, grad_scale, grad_gain, grad_shift)

time: 109 us -> 103 us (0.945)
  local copies, waits for them, and re-layouts: 8.54 us -> 0 us
  Pallas kernels: 99.1 us -> 103 us
    unnamed x20 -> x0, local copies, waits for them, and re-layouts: 8.54 us -> none
    pallas_call x1, Pallas kernels: 98 us -> 100 us  [per_device(): pl.pallas_call(whole_kernel, out_shape=(jax.ShapeDtypeStruct((4, 4, 16, S...]
    pallas_call x1, Pallas kernels: 1.07 us -> 2.33 us  [per_device(): pl.pallas_call(write_kernel, out_shape=tuple((jax.ShapeDtypeStruct(shape,...]
where the time goes in v2:
time: 103 us
  Pallas kernels  103 us (100%)
    pallas_call x1, Pallas kernels, per_device(): pl.pallas_call(whole_kernel, out_shape=(jax.ShapeDtypeStruct((4, 4, 16, S...  100 us
    pallas_call x1, Pallas kernels, per_device(): pl.pallas_call(write_kernel, out_shape=tuple((jax.ShapeDtypeStruct(shape,...  2.33 us

profile of v2, /device:TPU:1, one launch (start us, length us, event | category | flops | bytes accessed | tf_op | source)
XLA Modules:
  0.0 103.2 jit_solution(15788352345292844272)
XLA Ops:
  0.6 100.2 %shard_map.153 = (bf16[4,4,16,384]{3,2,1,0:T(8,128)(2,1)}, bf16[4,4,16,384]{3,2,1,0:T(8,128)(2,1)}, bf16[192,1536]{1,0:T(8,128)(2,1)}, f32[8,384]{1,0:T(8,128)}) custom-call(bf16[16,16,384]{2,1,0:T(8,128)(2,1)} %fields_hbm.1, bf16[16,16,384]{2,1,0:T(8,128)(2,1)} %cot_hbm.1, bf16[576,1536]{1,0:T(8,128)(2,1)} %bitcast.6, bf16[192,1536]{1,0:T(8,128)(2,1)} %wout.1, ...), custom_call_target="tpu_custom_call" | custom-call | flops 2000000000 | bytes 5000000 | tf_op jit(solution)/shard_map/pallas_call | solution.py:768
  100.9 2.3 %shard_map.154 = (bf16[16,16,384]{2,1,0:T(8,128)(2,1)}, bf16[16,16,384]{2,1,0:T(8,128)(2,1)}, bf16[192,1536]{1,0:T(8,128)(2,1)}, f32[3,225]{1,0:T(4,128)}, f32[3]{0:T(128)}, /*index=5*/f32[384]{0:T(512)}, f32[384]{0:T(512)}) custom-call(bf16[4,4,16,384]{3,2,1,0:T(8,128)(2,1)} %get-tuple-element.18.blocks_f, ...), custom_call_target="tpu_custom_call" | custom-call | flops 1000000 | bytes 2000000 | tf_op jit(solution)/shard_map/pallas_call | solution.py:795

commit v3 on v2

--- a/solution.py
+++ b/solution.py
@@ -237,15 +237,19 @@
             sent(chunk, base + 2 * n)
             sent(chunk, base + 3 * n)
 
-    def sum_start(name, part, recv, relay, g):
+    def sum_start(name, part, recv, relay, g, term):
         base = SLOTS[name] + g
+        part[far_edge, g] = term(far_edge)
 
         @pl.when(is_edge)
         def _():
             send(part.at[far_edge, g], relay.at[g], base + 6, on_line(partner), base + 4)
 
+        part[far_mid, g] = term(far_mid)
         send(part.at[far_mid, g], recv.at[t, g], base + 2 * far_slot, on_line(far_mid), base + 2)
+        part[partner, g] = term(partner)
         send(part.at[partner, g], recv.at[t, g], base, on_line(partner), base)
+        part[t, g] = term(t)
 
     def sum_relay(name, part, recv, relay, g):
         base = SLOTS[name] + g
@@ -379,8 +383,8 @@
             spread_wait("fields", 4, xbuf, w)
         proj = jnp.zeros((2 * CELLS, 3 * AW), F32)
         for src in range(4):
-            proj = proj + nt(xbuf[src, 2 * g:2 * g + 2].reshape(2 * CELLS, SH), wt[:, src * SH:(src + 1) * SH])
-        column = lab_col[2 * g * CELLS:2 * (g + 1) * CELLS]
+            proj = proj + nt(xbuf[src, pl.ds(2 * g, 2)].reshape(2 * CELLS, SH), wt[:, src * SH:(src + 1) * SH])
+        column = lab_col[pl.ds(pl.multiple_of(2 * g * CELLS, 128), 128), :]
         row = jnp.sum(jnp.where(eye, column, 0.0), axis=0, keepdims=True)
         same = row == column
         heads = range(HEADS)
@@ -424,7 +428,7 @@
         return jnp.concatenate([pair[:, :AW], pair[:, AW:]], axis=0)
 
     def cells_of(buf, g):
-        return buf[2 * g:2 * g + 2].reshape(2 * CELLS, SH).astype(F32)
+        return buf[pl.ds(2 * g, 2)].reshape(2 * CELLS, SH).astype(F32)
 
     def mix(g):
         spread_relay("att", 2, abuf, g)
@@ -456,13 +460,13 @@
         rows = cells_of(cbuf, g)
         grad = (inv_std * (rows * gain - grad_mean - normed * cross_mean)).astype(BF)
         gmix[g] = grad
-        for d in (2, 1, 3, 0):
-            dst = ring(t, d, 4)
-            part = nt(grad, wcol[(4 - d) % 4])
-            ga_send[dst, g] = jnp.concatenate([part[:CELLS], part[CELLS:]], axis=1).astype(BF)
-        sum_start("gatt", ga_send, ga_recv, ga_relay, g)
-        base = xbuf[t, 2 * g:2 * g + 2].reshape(2 * CELLS, SH).astype(F32)
-        obuf[2 * g:2 * g + 2] = (base + (gain * normed + shift)).astype(BF).reshape(2, 2, 2, 16, SH)
+        def term(dst):
+            part = nt(grad, wcol[ring(t - dst, 0, 4)])
+            return jnp.concatenate([part[:CELLS], part[CELLS:]], axis=1).astype(BF)
+
+        sum_start("gatt", ga_send, ga_recv, ga_relay, g, term)
+        base = xbuf[t, pl.ds(2 * g, 2)].reshape(2 * CELLS, SH).astype(F32)
+        obuf[pl.ds(2 * g, 2)] = (base + (gain * normed + shift)).astype(BF).reshape(2, 2, 2, 16, SH)
         gacc[0:1, :] += jnp.sum(rows * normed, axis=0, keepdims=True)
         gacc[1:2, :] += jnp.sum(rows, axis=0, keepdims=True)
 
@@ -492,14 +496,14 @@
         grads_q = [(gq[h] - q_float[h] * q_in[h]) * rqs[g, h] for h in heads]
         grads_k = [(gk[h] - k_float[h] * k_in[h]) * rks[g, h] for h in heads]
         stacked = jnp.concatenate(grads_q + grads_k + grads_v, axis=1).astype(BF)
-        for d in (2, 1, 3, 0):
-            dst = ring(t, d, 4)
-            gs_send[dst, g] = nn(stacked, wt[:, pl.ds(pl.multiple_of(dst * SH, 128), SH)]).astype(BF)
-        sum_start("gsh", gs_send, gs_recv, gs_relay, g)
+        def term(dst):
+            return nn(stacked, wt[:, pl.ds(pl.multiple_of(dst * SH, 128), SH)]).astype(BF)
+
+        sum_start("gsh", gs_send, gs_recv, gs_relay, g, term)
 
     def finish(g):
         total = sum_end("gsh", gs_send, gs_recv, g) + cells_of(cbuf, g)
-        gobuf[2 * g:2 * g + 2] = total.astype(BF).reshape(2, 2, 2, 16, SH)
+        gobuf[pl.ds(2 * g, 2)] = total.astype(BF).reshape(2, 2, 2, 16, SH)
 
     def give_first(buf, out, base):
         out[1:3, 1:3] = buf[0]
@@ -641,8 +645,14 @@
         out_s[1:2, TABLE:SH] = total[5:6, 128:256]
         out_s[2:5, 0:TABLE] = total[0:3]
 
-    forward(0)
-    forward(1)
+    def both(body):
+        def step(g, carry):
+            body(g)
+            return carry
+
+        lax.fori_loop(0, GROUPS, step, 0)
+
+    both(forward)
     own[11].wait()
     for o in range(15):
         y, x = plane_from(o)
@@ -655,59 +665,93 @@
         own[i].wait()
     for i in range(5):
         got(halo_parts(cbuf)[i], SLOTS["halo_c"] + i)
-    mix(0)
-    normalise(0)
-    mix(1)
-    sum_relay("gatt", ga_send, ga_recv, ga_relay, 0)
+    def drain_inputs():
+        for base, parts in (("halo_f", halo_parts(x_own)), ("halo_c", halo_parts(cbuf))):
+            for i in range(5):
+                sent(parts[i], SLOTS[base] + i)
+        for w in range(NWIN):
+            spread_drain("fields", 4, xbuf.at[0, 0], w)
+
+        @pl.when(has_piece)
+        def _():
+            for d in range(3):
+                sent(wcol.at[0, 0:48, 0:128], SLOTS["wcol_z"] + d)
+            for o in range(15):
+                sent(wcol.at[1:4, 0:48, 0:128], SLOTS["wcol_p"] + o)
+
+    def drain_middle():
+        for g in range(GROUPS):
+            spread_drain("att", 2, abuf.at[0, 0], g)
+            for i in range(3):
+                sent(stat_all.at[0, 0], SLOTS["stat"] + 2 * i + g)
+                sent(ga_send.at[0, 0], SLOTS["gatt"] + 2 * i + g)
+        sent(wc_send, SLOTS["w_core"])
+
+    def drain_late():
+        for i in range(5):
+            sent(back_parts(out_f)[i], SLOTS["out_f"] + i)
+        for o in range(15):
+            sent(sm_p.at[0], SLOTS["s_p"] + o)
+
+            @pl.when(plane(o)[0] < 3)
+            def _():
+                sent(wp_send.at[:, 0:16], SLOTS["w_p"] + o)
+
+    def middle(g):
+        mix(g)
+
+        @pl.when(g == 1)
+        def _():
+            sum_relay("gatt", ga_send, ga_recv, ga_relay, 0)
+
+        normalise(g)
+
+    both(middle)
     weight_first()
-    normalise(1)
     weight_start()
     sum_relay("gatt", ga_send, ga_recv, ga_relay, 1)
+    drain_inputs()
     give_first(obuf, out_f, SLOTS["out_f"])
     give_second(obuf, out_f, SLOTS["out_f"])
-    backward(0)
-    weight_plane()
-    backward(1)
-    sum_relay("gsh", gs_send, gs_recv, gs_relay, 0)
+
+    def last(g):
+        @pl.when(g == 1)
+        def _():
+            weight_plane()
+            sum_relay("gsh", gs_send, gs_recv, gs_relay, 0)
+
+        backward(g)
+
+    both(last)
     small_start()
     sum_relay("gsh", gs_send, gs_recv, gs_relay, 1)
-    weight_z()
+    drain_middle()
     finish(0)
     give_first(gobuf, out_g, SLOTS["out_g"])
+    weight_z()
     small_lat()
-    weight_back_plane()
+    drain_late()
     finish(1)
     give_second(gobuf, out_g, SLOTS["out_g"])
+    weight_back_plane()
+    small_end()
     weight_back_core()
-    small_end()
 
     for i in range(5):
         got(back_parts(out_f)[i], SLOTS["out_f"] + i)
         got(back_parts(out_g)[i], SLOTS["out_g"] + i)
 
-    for base, parts in (("halo_f", halo_parts(x_own)), ("halo_c", halo_parts(cbuf)),
-                        ("out_f", back_parts(out_f)), ("out_g", back_parts(out_g))):
-        for i in range(5):
-            sent(parts[i], SLOTS[base] + i)
-
-    for w in range(NWIN):
-        spread_drain("fields", 4, xbuf.at[0, 0], w)
+    for i in range(5):
+        sent(back_parts(out_g)[i], SLOTS["out_g"] + i)
     for g in range(GROUPS):
-        spread_drain("att", 2, abuf.at[0, 0], g)
         for i in range(3):
-            sent(stat_all.at[0, 0], SLOTS["stat"] + 2 * i + g)
-            sent(ga_send.at[0, 0], SLOTS["gatt"] + 2 * i + g)
             sent(gs_send.at[0, 0], SLOTS["gsh"] + 2 * i + g)
 
     @pl.when(has_piece)
     def _():
         for d in range(3):
-            sent(wcol.at[0, 0:48, 0:128], SLOTS["wcol_z"] + d)
             for j in (0, 1):
                 sent(wp_sum.at[j], SLOTS["w_zs"] + 4 * j + d + 1)
-        for o in range(15):
-            sent(wcol.at[1:4, 0:48, 0:128], SLOTS["wcol_p"] + o)
-
         for j in (0, 1):
             @pl.when(2 * core + j != t)
             def _():
@@ -719,21 +763,17 @@
             sent(out_w.at[0:16], SLOTS["back_p"] + o)
         sent(out_w.at[0:16], SLOTS["back_core"] + lx * 3 + ly)
 
-    for o in range(15):
-        sent(sm_p.at[0], SLOTS["s_p"] + o)
-
-        @pl.when(plane(o)[0] < 3)
-        def _():
-            sent(wp_send.at[:, 0:16], SLOTS["w_p"] + o)
-
-        @pl.when(holder & (plane_from(o)[0] < 3))
-        def _():
+    @pl.when(holder)
+    def _():
+        for o in range(15):
             y, x = plane_from(o)
-            sent(out_w.at[0:16], SLOTS["back_core"] + x * 3 + y)
+
+            @pl.when(y < 3)
+            def _():
+                sent(out_w.at[0:16], SLOTS["back_core"] + x * 3 + y)
 
     for d in range(7):
         sent(sm_l.at[0], SLOTS["s_l"] + d)
-    sent(wc_send, SLOTS["w_core"])
 
     @pl.when(jnp.logical_not(holder))
     def _():

time: 103 us -> 105 us (1.019)
  Pallas kernels: 103 us -> 105 us
    pallas_call x1, Pallas kernels: 100 us -> 102 us  [per_device(): pl.pallas_call(whole_kernel, out_shape=(jax.ShapeDtypeStruct((4, 4, 16, S...]
where the time goes in v3:
time: 105 us
  Pallas kernels  105 us (100%)
    pallas_call x1, Pallas kernels, per_device(): pl.pallas_call(whole_kernel, out_shape=(jax.ShapeDtypeStruct((4, 4, 16, S...  102 us
    pallas_call x1, Pallas kernels, per_device(): pl.pallas_call(write_kernel, out_shape=tuple((jax.ShapeDtypeStruct(shape,...  2.33 us

profile of v3, /device:TPU:1, one launch (start us, length us, event | category | flops | bytes accessed | tf_op | source)
XLA Modules:
  0.0 105.2 jit_solution(7374787890818048135)
XLA Ops:
  0.6 102.2 %shard_map.153 = (bf16[4,4,16,384]{3,2,1,0:T(8,128)(2,1)}, bf16[4,4,16,384]{3,2,1,0:T(8,128)(2,1)}, bf16[192,1536]{1,0:T(8,128)(2,1)}, f32[8,384]{1,0:T(8,128)}) custom-call(bf16[16,16,384]{2,1,0:T(8,128)(2,1)} %fields_hbm.1, bf16[16,16,384]{2,1,0:T(8,128)(2,1)} %cot_hbm.1, bf16[576,1536]{1,0:T(8,128)(2,1)} %bitcast.6, bf16[192,1536]{1,0:T(8,128)(2,1)} %wout.1, ...), custom_call_target="tpu_custom_call" | custom-call | flops 2000000000 | bytes 5000000 | tf_op jit(solution)/shard_map/pallas_call | solution.py:808
  102.8 2.3 %shard_map.154 = (bf16[16,16,384]{2,1,0:T(8,128)(2,1)}, bf16[16,16,384]{2,1,0:T(8,128)(2,1)}, bf16[192,1536]{1,0:T(8,128)(2,1)}, f32[3,225]{1,0:T(4,128)}, f32[3]{0:T(128)}, /*index=5*/f32[384]{0:T(512)}, f32[384]{0:T(512)}) custom-call(bf16[4,4,16,384]{3,2,1,0:T(8,128)(2,1)} %get-tuple-element.18.blocks_f, ...), custom_call_target="tpu_custom_call" | custom-call | flops 1000000 | bytes 2000000 | tf_op jit(solution)/shard_map/pallas_call | solution.py:835

commit v4 on v3

--- a/solution.py
+++ b/solution.py
@@ -25,8 +25,8 @@
 COUNT = 0
 for _name, _n in (
     ("halo_f", 5), ("halo_c", 5), ("fields", 16), ("wcol_z", 3), ("wcol_p", 15), ("att", 8), ("stat", 6),
-    ("gatt", 8), ("gsh", 8), ("out_f", 5), ("out_g", 5), ("w_core", 1), ("w_p", 15), ("w_z", 16),
-    ("w_zs", 8), ("back_p", 15), ("back_core", 12), ("s_p", 15), ("s_l", 7),
+    ("gatt", 8), ("gsh", 8), ("out_f", 5), ("out_g", 5), ("w_core", 1), ("w_p", 15), ("w_pair", 1), ("w_z", 8),
+    ("w_zs", 4), ("back_p", 15), ("back_core", 12), ("s_p", 15), ("s_l", 3), ("s_far", 1),
 ):
     SLOTS[_name] = COUNT
     COUNT += _n
@@ -100,7 +100,7 @@
     out_f, out_g, out_w, out_s,
     fields_grid, cot_grid, wt, fields, cot, xbuf, cbuf, wcol, abuf, onehot, bsrow, idx_row, tab_pad, bsig, lab_col, qs, ks, vs, probs, coss, rqs, rks,
     mixed, stat_all, gmix, ga_send, ga_recv, ga_relay, gs_send, gs_recv, gs_relay, obuf, gobuf, tacc, sacc, gacc, flat,
-    wc_send, wc_recv, wacc, wp_send, wp_recv, wp_sum, bz, sm_p, sm_l, local_sem, ssem, rsem,
+    wc_send, wc_recv, wacc, wp_send, wp_recv, wp_sum, wp_pair, wp_both, bz, sm_p, sm_l, sm_f, local_sem, ssem, rsem,
 ):
     lat = lax.axis_index("lat")
     lon = lax.axis_index("lon")
@@ -158,9 +158,13 @@
     keep(cot_hbm, cot_grid)
     keep(wt_hbm, wt)
 
-    partners = [plane_dev(o) for o in range(15)] + [(ring(lat, d, 8), lon, t) for d in range(1, 8)]
-    partners += [(lat_p, lon_p, t), (lat_n, lon_n, t)] + [tp_dev(d) for d in (1, 2, 3)]
-    partners += [(ring(zh, dz, 4) * 2 + core, lon, ring(t, dt, 4)) for dz in (1, 2, 3) for dt in (1, 2, 3)]
+    z_pair = zh + 1 - 2 * (zh % 2)
+    z_far = 3 - zh
+    pair_devs = [sib, (z_pair * 2 + core, lon, t), (z_pair * 2 + (1 - core), lon, t)]
+
+    partners = [plane_dev(o) for o in range(15)] + pair_devs
+    partners += [(lat_p, lon, t), (lat_n, lon, t), (lat_p, lon_p, t), (lat_n, lon_n, t)]
+    partners += [tp_dev(d) for d in (1, 2, 3)] + [(z_far * 2 + core, lon, ring(t, d, 4)) for d in range(4)]
     barrier = pltpu.get_barrier_semaphore()
     for dev in partners:
         pl.semaphore_signal(barrier, inc=1, device_id=dev, device_id_type=MESH)
@@ -562,28 +566,34 @@
                 for o in range(15):
                     total = total + wp_recv[o, j].astype(F32)
                 wp_sum[j] = total.astype(BF)
+            send(wp_sum, wp_pair, SLOTS["w_pair"], (z_pair * 2 + core, lon, t))
+
+    def weight_far():
+        @pl.when(has_piece)
+        def _():
+            got(wp_pair, SLOTS["w_pair"])
+            wp_both[...] = (wp_sum[...].astype(F32) + wp_pair[...].astype(F32)).astype(BF)
             for j in (0, 1):
                 keeper = 2 * core + j
-                for dz in range(4):
-                    @pl.when((keeper != t) if dz == 0 else (keeper >= 0))
-                    def _():
-                        dev = (ring(zh, dz, 4) * 2 + core, lon, keeper)
-                        send(wp_sum.at[j], bz.at[zh, t], SLOTS["w_z"] + zh * 4 + t, dev, SLOTS["w_zs"] + 4 * j + dz)
+                slot = SLOTS["w_z"] + (zh // 2) * 4 + t
+                send(wp_both.at[j], bz.at[zh // 2, t], slot, (z_far * 2 + core, lon, keeper), SLOTS["w_zs"] + 2 * j)
+
+                @pl.when(keeper != t)
+                def _():
+                    send(wp_both.at[j], bz.at[zh // 2, t], slot, (lat, lon, keeper), SLOTS["w_zs"] + 2 * j + 1)
 
     def weight_back_plane():
         @pl.when(holder & has_piece)
         def _():
-            bz[zh, t] = wp_sum[t % 2]
-            for z in range(4):
+            bz[zh // 2, t] = wp_both[t % 2]
+            for z in range(2):
                 for src in range(4):
-                    @pl.when((zh != z) | (t != src))
+                    @pl.when((zh // 2 != z) | (t != src))
                     def _():
                         got(bz.at[z, src], SLOTS["w_z"] + z * 4 + src)
 
             for src in range(4):
-                total = bz[0, src].astype(F32)
-                for z in range(1, 4):
-                    total = total + bz[z, src].astype(F32)
+                total = bz[0, src].astype(F32) + bz[1, src].astype(F32)
                 out_w[rows_of(ly, lx), src * SH:(src + 1) * SH] = total.astype(BF)
             mine = out_w.at[rows_of(ly, lx)]
             for o in range(15):
@@ -629,16 +639,20 @@
         total = sm_p[0]
         for i in range(1, 16):
             total = total + sm_p[i]
-        sm_l[lat] = total
-        for d in range(1, 8):
-            send(sm_l.at[lat], sm_l.at[lat], SLOTS["s_l"] + d - 1, (ring(lat, d, 8), lon, t))
+        sm_l[2 * (zh % 2) + core] = total
+        mine = sm_l.at[2 * (zh % 2) + core]
+        for i, dev in enumerate(pair_devs):
+            send(mine, mine, SLOTS["s_l"] + i, dev)
+
+    def small_far():
+        for i, where in enumerate((2 * (zh % 2) + 1 - core, 2 * (1 - zh % 2) + core, 2 * (1 - zh % 2) + 1 - core)):
+            got(sm_l.at[where], SLOTS["s_l"] + i)
+        sm_f[0] = sm_l[0] + sm_l[1] + sm_l[2] + sm_l[3]
+        send(sm_f.at[0], sm_f.at[1], SLOTS["s_far"], (z_far * 2 + core, lon, t))
 
     def small_end():
-        for d in range(1, 8):
-            got(sm_l.at[ring(lat, -d, 8)], SLOTS["s_l"] + d - 1)
-        total = sm_l[0]
-        for i in range(1, 8):
-            total = total + sm_l[i]
+        got(sm_f.at[1], SLOTS["s_far"])
+        total = sm_f[0] + sm_f[1]
         out_s[...] = jnp.zeros_like(out_s)
         out_s[0:2, 0:TABLE] = total[3:5]
         out_s[0:1, TABLE:SH] = total[5:6, 0:128]
@@ -723,19 +737,21 @@
         backward(g)
 
     both(last)
+    weight_z()
     small_start()
     sum_relay("gsh", gs_send, gs_recv, gs_relay, 1)
+    weight_far()
     drain_middle()
     finish(0)
     give_first(gobuf, out_g, SLOTS["out_g"])
-    weight_z()
     small_lat()
+    weight_back_plane()
+    small_far()
     drain_late()
     finish(1)
     give_second(gobuf, out_g, SLOTS["out_g"])
-    weight_back_plane()
+    weight_back_core()
     small_end()
-    weight_back_core()
 
     for i in range(5):
         got(back_parts(out_f)[i], SLOTS["out_f"] + i)
@@ -749,13 +765,13 @@
 
     @pl.when(has_piece)
     def _():
-        for d in range(3):
-            for j in (0, 1):
-                sent(wp_sum.at[j], SLOTS["w_zs"] + 4 * j + d + 1)
+        sent(wp_sum, SLOTS["w_pair"])
         for j in (0, 1):
+            sent(wp_both.at[j], SLOTS["w_zs"] + 2 * j)
+
             @pl.when(2 * core + j != t)
             def _():
-                sent(wp_sum.at[j], SLOTS["w_zs"] + 4 * j)
+                sent(wp_both.at[j], SLOTS["w_zs"] + 2 * j + 1)
 
     @pl.when(holder & has_piece)
     def _():
@@ -772,8 +788,9 @@
             def _():
                 sent(out_w.at[0:16], SLOTS["back_core"] + x * 3 + y)
 
-    for d in range(7):
-        sent(sm_l.at[0], SLOTS["s_l"] + d)
+    for i in range(3):
+        sent(sm_l.at[0], SLOTS["s_l"] + i)
+    sent(sm_f.at[0], SLOTS["s_far"])
 
     @pl.when(jnp.logical_not(holder))
     def _():
@@ -802,8 +819,8 @@
         ((4, 2, 2, 16, SH), BF), ((4, 2, 2, 16, SH), BF),
         ((HEADS, 2 * CELLS, 2 * CELLS), F32), ((HEADS, 2 * CELLS, 2 * CELLS), F32), ((8, SH), F32), ((8, NPAIR), F32),
         ((2, AW, SH), BF), ((2, AW, SH), BF), ((4, AW, SH), F32),
-        ((2, AW, SH), BF), ((15, 2, 16, SH), BF), ((2, 16, SH), BF), ((4, 4, 16, SH), BF),
-        ((16, 8, TABLE), F32), ((8, 8, TABLE), F32),
+        ((2, AW, SH), BF), ((15, 2, 16, SH), BF), ((2, 16, SH), BF), ((2, 16, SH), BF), ((2, 16, SH), BF),
+        ((2, 4, 16, SH), BF), ((16, 8, TABLE), F32), ((4, 8, TABLE), F32), ((2, 8, TABLE), F32),
     ]
     out_f, out_g, out_w, out_s = pl.pallas_call(
         whole_kernel,

time: 105 us -> 102 us (0.971)
  Pallas kernels: 105 us -> 101 us
    pallas_call x1, Pallas kernels: 102 us -> 98.3 us  [per_device(): pl.pallas_call(whole_kernel, out_shape=(jax.ShapeDtypeStruct((4, 4, 16, S...]
where the time goes in v4:
time: 102 us; the launch traced here: 101 us
  Pallas kernels  101 us (99%)
    pallas_call x1, Pallas kernels, per_device(): pl.pallas_call(whole_kernel, out_shape=(jax.ShapeDtypeStruct((4, 4, 16, S...  98.3 us
    pallas_call x1, Pallas kernels, per_device(): pl.pallas_call(write_kernel, out_shape=tuple((jax.ShapeDtypeStruct(shape,...  2.33 us

profile of v4, /device:TPU:1, one launch (start us, length us, event | category | flops | bytes accessed | tf_op | source)
XLA Modules:
  0.0 101.3 jit_solution(9932278128911797640)
XLA Ops:
  0.6 98.3 %shard_map.153 = (bf16[4,4,16,384]{3,2,1,0:T(8,128)(2,1)}, bf16[4,4,16,384]{3,2,1,0:T(8,128)(2,1)}, bf16[192,1536]{1,0:T(8,128)(2,1)}, f32[8,384]{1,0:T(8,128)}) custom-call(bf16[16,16,384]{2,1,0:T(8,128)(2,1)} %fields_hbm.1, bf16[16,16,384]{2,1,0:T(8,128)(2,1)} %cot_hbm.1, bf16[576,1536]{1,0:T(8,128)(2,1)} %bitcast.6, bf16[192,1536]{1,0:T(8,128)(2,1)} %wout.1, ...), custom_call_target="tpu_custom_call" | custom-call | flops 2000000000 | bytes 5000000 | tf_op jit(solution)/shard_map/pallas_call | solution.py:825
  99.0 2.3 %shard_map.154 = (bf16[16,16,384]{2,1,0:T(8,128)(2,1)}, bf16[16,16,384]{2,1,0:T(8,128)(2,1)}, bf16[192,1536]{1,0:T(8,128)(2,1)}, f32[3,225]{1,0:T(4,128)}, f32[3]{0:T(128)}, /*index=5*/f32[384]{0:T(512)}, f32[384]{0:T(512)}) custom-call(bf16[4,4,16,384]{3,2,1,0:T(8,128)(2,1)} %get-tuple-element.18.blocks_f, ...), custom_call_target="tpu_custom_call" | custom-call | flops 1000000 | bytes 2000000 | tf_op jit(solution)/shard_map/pallas_call | solution.py:852

commit v5 on v4

--- a/solution.py
+++ b/solution.py
@@ -182,10 +182,12 @@
 
     pl.semaphore_wait(barrier, len(partners))
 
-    def halo(grid, dst, base):
+    def halo_lon(grid, dst, base):
         send(grid.at[1:3, 0], dst.at[1, :, 1], base, (lat, lon_p, t))
+        send(grid.at[3, 0], dst.at[3, 0, 1], base + 2, (lat, lon_p, t))
+
+    def halo_lat(grid, dst, base):
         send(grid.at[0, 1:3], dst.at[2, 1], base + 1, (lat_p, lon, t))
-        send(grid.at[3, 0], dst.at[3, 0, 1], base + 2, (lat, lon_p, t))
         send(grid.at[0, 3], dst.at[3, 1, 0], base + 3, (lat_p, lon, t))
         send(grid.at[0, 0], dst.at[3, 1, 1], base + 4, (lat_p, lon_p, t))
 
@@ -285,7 +287,8 @@
     def give_fields(w, src):
         spread_start("fields", 4, src, x_own.at[w], w)
 
-    halo(fields, x_own, SLOTS["halo_f"])
+    halo_lat(fields, x_own, SLOTS["halo_f"])
+    halo_lon(fields, x_own, SLOTS["halo_f"])
 
     piece_rows = pl.ds(pl.multiple_of(lx * 48, 16), 48)
     has_piece = ly < 3
@@ -350,7 +353,7 @@
         for o in range(15):
             send(piece(ly, lx), piece(ly, lx), SLOTS["wcol_p"] + o, plane_dev(o))
 
-    halo(cot, cbuf, SLOTS["halo_c"])
+    halo_lon(cot, cbuf, SLOTS["halo_c"])
 
     tab_pad[...] = jnp.zeros_like(tab_pad)
     tab_pad[0:HEADS, 0:table.shape[1]] = table[...]
@@ -381,13 +384,25 @@
     eye = iota((2 * CELLS, 2 * CELLS), 0) == iota((2 * CELLS, 2 * CELLS), 1)
 
     def forward(g):
-        for w in (2 * g, 2 * g + 1):
-            spread_relay("fields", 4, xbuf, w)
+        @pl.when(g == 0)
+        def _():
+            spread_relay("fields", 4, xbuf, 0)
+            spread_relay("fields", 4, xbuf, 1)
+
+        @pl.when(g == 1)
+        def _():
+            spread_relay("fields", 4, xbuf, 3)
+
         for w in (2 * g, 2 * g + 1):
             spread_wait("fields", 4, xbuf, w)
         proj = jnp.zeros((2 * CELLS, 3 * AW), F32)
         for src in range(4):
             proj = proj + nt(xbuf[src, pl.ds(2 * g, 2)].reshape(2 * CELLS, SH), wt[:, src * SH:(src + 1) * SH])
+
+        @pl.when(g == 0)
+        def _():
+            spread_relay("fields", 4, xbuf, 2)
+
         column = lab_col[pl.ds(pl.multiple_of(2 * g * CELLS, 128), 128), :]
         row = jnp.sum(jnp.where(eye, column, 0.0), axis=0, keepdims=True)
         same = row == column
@@ -666,7 +681,14 @@
 
         lax.fori_loop(0, GROUPS, step, 0)
 
-    both(forward)
+    def first(g):
+        forward(g)
+
+        @pl.when(g == 0)
+        def _():
+            halo_lat(cot, cbuf, SLOTS["halo_c"])
+
+    both(first)
     own[11].wait()
     for o in range(15):
         y, x = plane_from(o)
@@ -677,8 +699,8 @@
 
     for i in (7, 8, 9, 10):
         own[i].wait()
-    for i in range(5):
-        got(halo_parts(cbuf)[i], SLOTS["halo_c"] + i)
+    got(halo_parts(cbuf)[0], SLOTS["halo_c"])
+
     def drain_inputs():
         for base, parts in (("halo_f", halo_parts(x_own)), ("halo_c", halo_parts(cbuf))):
             for i in range(5):
@@ -712,35 +734,40 @@
                 sent(wp_send.at[:, 0:16], SLOTS["w_p"] + o)
 
     def middle(g):
+        @pl.when(g == 1)
+        def _():
+            for i in range(1, 5):
+                got(halo_parts(cbuf)[i], SLOTS["halo_c"] + i)
+
         mix(g)
 
         @pl.when(g == 1)
         def _():
             sum_relay("gatt", ga_send, ga_recv, ga_relay, 0)
+            weight_first()
 
         normalise(g)
 
     both(middle)
-    weight_first()
     weight_start()
     sum_relay("gatt", ga_send, ga_recv, ga_relay, 1)
-    drain_inputs()
-    give_first(obuf, out_f, SLOTS["out_f"])
-    give_second(obuf, out_f, SLOTS["out_f"])
 
     def last(g):
         @pl.when(g == 1)
         def _():
             weight_plane()
             sum_relay("gsh", gs_send, gs_recv, gs_relay, 0)
+            give_first(obuf, out_f, SLOTS["out_f"])
+            give_second(obuf, out_f, SLOTS["out_f"])
 
         backward(g)
 
     both(last)
     weight_z()
+    sum_relay("gsh", gs_send, gs_recv, gs_relay, 1)
     small_start()
-    sum_relay("gsh", gs_send, gs_recv, gs_relay, 1)
     weight_far()
+    drain_inputs()
     drain_middle()
     finish(0)
     give_first(gobuf, out_g, SLOTS["out_g"])

time: 102 us -> 99 us (0.971)
  Pallas kernels: 101 us -> 98.1 us
    pallas_call x1, Pallas kernels: 98.3 us -> 95.8 us  [per_device(): pl.pallas_call(whole_kernel, out_shape=(jax.ShapeDtypeStruct((4, 4, 16, S...]
where the time goes in v5:
time: 99 us; the launch traced here: 98.8 us
  Pallas kernels  98.1 us (99%)
    pallas_call x1, Pallas kernels, per_device(): pl.pallas_call(whole_kernel, out_shape=(jax.ShapeDtypeStruct((4, 4, 16, S...  95.8 us
    pallas_call x1, Pallas kernels, per_device(): pl.pallas_call(write_kernel, out_shape=tuple((jax.ShapeDtypeStruct(shape,...  2.33 us

profile of v5, /device:TPU:1, one launch (start us, length us, event | category | flops | bytes accessed | tf_op | source)
XLA Modules:
  0.0 98.8 jit_solution(3988840740649421345)
XLA Ops:
  0.6 95.8 %shard_map.153 = (bf16[4,4,16,384]{3,2,1,0:T(8,128)(2,1)}, bf16[4,4,16,384]{3,2,1,0:T(8,128)(2,1)}, bf16[192,1536]{1,0:T(8,128)(2,1)}, f32[8,384]{1,0:T(8,128)}) custom-call(bf16[16,16,384]{2,1,0:T(8,128)(2,1)} %fields_hbm.1, bf16[16,16,384]{2,1,0:T(8,128)(2,1)} %cot_hbm.1, bf16[576,1536]{1,0:T(8,128)(2,1)} %bitcast.6, bf16[192,1536]{1,0:T(8,128)(2,1)} %wout.1, ...), custom_call_target="tpu_custom_call" | custom-call | flops 2000000000 | bytes 5000000 | tf_op jit(solution)/shard_map/pallas_call | solution.py:852
  96.5 2.3 %shard_map.154 = (bf16[16,16,384]{2,1,0:T(8,128)(2,1)}, bf16[16,16,384]{2,1,0:T(8,128)(2,1)}, bf16[192,1536]{1,0:T(8,128)(2,1)}, f32[3,225]{1,0:T(4,128)}, f32[3]{0:T(128)}, /*index=5*/f32[384]{0:T(512)}, f32[384]{0:T(512)}) custom-call(bf16[4,4,16,384]{3,2,1,0:T(8,128)(2,1)} %get-tuple-element.18.blocks_f, ...), custom_call_target="tpu_custom_call" | custom-call | flops 1000000 | bytes 2000000 | tf_op jit(solution)/shard_map/pallas_call | solution.py:879

commit v6 on v5

--- a/solution.py
+++ b/solution.py
@@ -354,6 +354,8 @@
             send(piece(ly, lx), piece(ly, lx), SLOTS["wcol_p"] + o, plane_dev(o))
 
     halo_lon(cot, cbuf, SLOTS["halo_c"])
+
+    spread_relay("fields", 4, xbuf, 0)
 
     tab_pad[...] = jnp.zeros_like(tab_pad)
     tab_pad[0:HEADS, 0:table.shape[1]] = table[...]
@@ -373,6 +375,7 @@
                 pair = jnp.concatenate([16.0 * sig[h:h + 1, k * CELLS:(k + 1) * CELLS]] * 2, axis=1)
                 bsig[h, at:at + 1, :] = pair
                 bsig[h, CELLS + at:CELLS + at + 1, :] = pair
+    spread_relay("fields", 4, xbuf, 1)
     tacc[...] = jnp.zeros_like(tacc)
     sacc[...] = jnp.zeros_like(sacc)
     gacc[...] = jnp.zeros_like(gacc)
@@ -384,11 +387,6 @@
     eye = iota((2 * CELLS, 2 * CELLS), 0) == iota((2 * CELLS, 2 * CELLS), 1)
 
     def forward(g):
-        @pl.when(g == 0)
-        def _():
-            spread_relay("fields", 4, xbuf, 0)
-            spread_relay("fields", 4, xbuf, 1)
-
         @pl.when(g == 1)
         def _():
             spread_relay("fields", 4, xbuf, 3)
@@ -450,7 +448,6 @@
         return buf[pl.ds(2 * g, 2)].reshape(2 * CELLS, SH).astype(F32)
 
     def mix(g):
-        spread_relay("att", 2, abuf, g)
         spread_wait("att", 2, abuf, g)
         total = jnp.zeros((2 * CELLS, SH), F32)
         for d in range(4):
@@ -739,7 +736,15 @@
             for i in range(1, 5):
                 got(halo_parts(cbuf)[i], SLOTS["halo_c"] + i)
 
+        @pl.when(g == 0)
+        def _():
+            spread_relay("att", 2, abuf, 0)
+
         mix(g)
+
+        @pl.when(g == 0)
+        def _():
+            spread_relay("att", 2, abuf, 1)
 
         @pl.when(g == 1)
         def _():

time: 99 us -> 96.5 us (0.975)
  Pallas kernels: 98.1 us -> 95.7 us
    pallas_call x1, Pallas kernels: 95.8 us -> 93.3 us  [per_device(): pl.pallas_call(whole_kernel, out_shape=(jax.ShapeDtypeStruct((4, 4, 16, S...]
where the time goes in v6:
time: 96.5 us; the launch traced here: 96.3 us
  Pallas kernels  95.7 us (99%)
    pallas_call x1, Pallas kernels, per_device(): pl.pallas_call(whole_kernel, out_shape=(jax.ShapeDtypeStruct((4, 4, 16, S...  93.3 us
    pallas_call x1, Pallas kernels, per_device(): pl.pallas_call(write_kernel, out_shape=tuple((jax.ShapeDtypeStruct(shape,...  2.33 us

profile of v6, /device:TPU:1, one launch (start us, length us, event | category | flops | bytes accessed | tf_op | source)
XLA Modules:
  0.0 96.3 jit_solution(10999728442774223895)
XLA Ops:
  0.6 93.3 %shard_map.153 = (bf16[4,4,16,384]{3,2,1,0:T(8,128)(2,1)}, bf16[4,4,16,384]{3,2,1,0:T(8,128)(2,1)}, bf16[192,1536]{1,0:T(8,128)(2,1)}, f32[8,384]{1,0:T(8,128)}) custom-call(bf16[16,16,384]{2,1,0:T(8,128)(2,1)} %fields_hbm.1, bf16[16,16,384]{2,1,0:T(8,128)(2,1)} %cot_hbm.1, bf16[576,1536]{1,0:T(8,128)(2,1)} %bitcast.6, bf16[192,1536]{1,0:T(8,128)(2,1)} %wout.1, ...), custom_call_target="tpu_custom_call" | custom-call | flops 2000000000 | bytes 5000000 | tf_op jit(solution)/shard_map/pallas_call | solution.py:857
  94.0 2.3 %shard_map.154 = (bf16[16,16,384]{2,1,0:T(8,128)(2,1)}, bf16[16,16,384]{2,1,0:T(8,128)(2,1)}, bf16[192,1536]{1,0:T(8,128)(2,1)}, f32[3,225]{1,0:T(4,128)}, f32[3]{0:T(128)}, /*index=5*/f32[384]{0:T(512)}, f32[384]{0:T(512)}) custom-call(bf16[4,4,16,384]{3,2,1,0:T(8,128)(2,1)} %get-tuple-element.18.blocks_f, ...), custom_call_target="tpu_custom_call" | custom-call | flops 1000000 | bytes 2000000 | tf_op jit(solution)/shard_map/pallas_call | solution.py:884

commit v7 on v6

--- a/solution.py
+++ b/solution.py
@@ -224,14 +224,18 @@
             got(chunk, base + 2 * n)
             send(chunk, chunk, base + 2 * n, on_line(partner), base + 3 * n)
 
-    def spread_wait(name, n, buf, i):
+    due = (t, partner, far_mid, far_edge)
+
+    def spread_wait(name, n, buf, i, step):
         base = SLOTS[name] + i
-        got(buf.at[partner, i], base)
-        got(buf.at[far_mid, i], base + n)
-
-        @pl.when(is_edge)
-        def _():
-            got(buf.at[far_edge, i], base + 2 * n)
+        if step == 1:
+            got(buf.at[partner, i], base)
+        if step == 2:
+            got(buf.at[far_mid, i], base + n)
+        if step == 3:
+            @pl.when(is_edge)
+            def _():
+                got(buf.at[far_edge, i], base + 2 * n)
 
     def spread_drain(name, n, chunk, i):
         base = SLOTS[name] + i
@@ -391,11 +395,12 @@
         def _():
             spread_relay("fields", 4, xbuf, 3)
 
-        for w in (2 * g, 2 * g + 1):
-            spread_wait("fields", 4, xbuf, w)
         proj = jnp.zeros((2 * CELLS, 3 * AW), F32)
-        for src in range(4):
-            proj = proj + nt(xbuf[src, pl.ds(2 * g, 2)].reshape(2 * CELLS, SH), wt[:, src * SH:(src + 1) * SH])
+        for step, src in enumerate(due):
+            for w in (2 * g, 2 * g + 1):
+                spread_wait("fields", 4, xbuf, w, step)
+            cols = pl.ds(pl.multiple_of(src * SH, 128), SH)
+            proj = proj + nt(xbuf[src, pl.ds(2 * g, 2)].reshape(2 * CELLS, SH), wt[:, cols])
 
         @pl.when(g == 0)
         def _():
@@ -448,10 +453,10 @@
         return buf[pl.ds(2 * g, 2)].reshape(2 * CELLS, SH).astype(F32)
 
     def mix(g):
-        spread_wait("att", 2, abuf, g)
         total = jnp.zeros((2 * CELLS, SH), F32)
-        for d in range(4):
-            total = total + nn(unpack(abuf[ring(t, -d, 4), g]), wcol[d])
+        for step, src in enumerate(due):
+            spread_wait("att", 2, abuf, g, step)
+            total = total + nn(unpack(abuf[src, g]), wcol[ring(t - src, 0, 4)])
         mixed[g] = total
         grad_norm = cells_of(cbuf, g) * gain
         packed = jnp.zeros((2 * CELLS, 128), F32)

time: 96.5 us -> 96.3 us (level)
  no operation moved by 1% of the time
where the time goes in v7:
time: 96.3 us; the launch traced here: 96.1 us
  Pallas kernels  95.4 us (99%)
    pallas_call x1, Pallas kernels, per_device(): pl.pallas_call(whole_kernel, out_shape=(jax.ShapeDtypeStruct((4, 4, 16, S...  93.1 us
    pallas_call x1, Pallas kernels, per_device(): pl.pallas_call(write_kernel, out_shape=tuple((jax.ShapeDtypeStruct(shape,...  2.33 us

profile of v7, /device:TPU:1, one launch (start us, length us, event | category | flops | bytes accessed | tf_op | source)
XLA Modules:
  0.0 96.1 jit_solution(6849466785425986026)
XLA Ops:
  0.6 93.1 %shard_map.153 = (bf16[4,4,16,384]{3,2,1,0:T(8,128)(2,1)}, bf16[4,4,16,384]{3,2,1,0:T(8,128)(2,1)}, bf16[192,1536]{1,0:T(8,128)(2,1)}, f32[8,384]{1,0:T(8,128)}) custom-call(bf16[16,16,384]{2,1,0:T(8,128)(2,1)} %fields_hbm.1, bf16[16,16,384]{2,1,0:T(8,128)(2,1)} %cot_hbm.1, bf16[576,1536]{1,0:T(8,128)(2,1)} %bitcast.6, bf16[192,1536]{1,0:T(8,128)(2,1)} %wout.1, ...), custom_call_target="tpu_custom_call" | custom-call | flops 2000000000 | bytes 5000000 | tf_op jit(solution)/shard_map/pallas_call | solution.py:862
  93.8 2.3 %shard_map.154 = (bf16[16,16,384]{2,1,0:T(8,128)(2,1)}, bf16[16,16,384]{2,1,0:T(8,128)(2,1)}, bf16[192,1536]{1,0:T(8,128)(2,1)}, f32[3,225]{1,0:T(4,128)}, f32[3]{0:T(128)}, /*index=5*/f32[384]{0:T(512)}, f32[384]{0:T(512)}) custom-call(bf16[4,4,16,384]{3,2,1,0:T(8,128)(2,1)} %get-tuple-element.18.blocks_f, ...), custom_call_target="tpu_custom_call" | custom-call | flops 1000000 | bytes 2000000 | tf_op jit(solution)/shard_map/pallas_call | solution.py:889

commit v8 on v7

--- a/solution.py
+++ b/solution.py
@@ -777,16 +777,16 @@
     sum_relay("gsh", gs_send, gs_recv, gs_relay, 1)
     small_start()
     weight_far()
-    drain_inputs()
-    drain_middle()
     finish(0)
     give_first(gobuf, out_g, SLOTS["out_g"])
     small_lat()
     weight_back_plane()
-    small_far()
-    drain_late()
     finish(1)
     give_second(gobuf, out_g, SLOTS["out_g"])
+    small_far()
+    drain_inputs()
+    drain_middle()
+    drain_late()
     weight_back_core()
     small_end()
 

time: 96.3 us -> 96.8 us (level)
  no operation moved by 1% of the time
where the time goes in v8:
time: 96.8 us; the launch traced here: 96.6 us
  Pallas kernels  95.9 us (99%)
    pallas_call x1, Pallas kernels, per_device(): pl.pallas_call(whole_kernel, out_shape=(jax.ShapeDtypeStruct((4, 4, 16, S...  93.6 us
    pallas_call x1, Pallas kernels, per_device(): pl.pallas_call(write_kernel, out_shape=tuple((jax.ShapeDtypeStruct(shape,...  2.33 us

profile of v8, /device:TPU:1, one launch (start us, length us, event | category | flops | bytes accessed | tf_op | source)
XLA Modules:
  0.0 96.6 jit_solution(997464371488354265)
XLA Ops:
  0.6 93.6 %shard_map.153 = (bf16[4,4,16,384]{3,2,1,0:T(8,128)(2,1)}, bf16[4,4,16,384]{3,2,1,0:T(8,128)(2,1)}, bf16[192,1536]{1,0:T(8,128)(2,1)}, f32[8,384]{1,0:T(8,128)}) custom-call(bf16[16,16,384]{2,1,0:T(8,128)(2,1)} %fields_hbm.1, bf16[16,16,384]{2,1,0:T(8,128)(2,1)} %cot_hbm.1, bf16[576,1536]{1,0:T(8,128)(2,1)} %bitcast.6, bf16[192,1536]{1,0:T(8,128)(2,1)} %wout.1, ...), custom_call_target="tpu_custom_call" | custom-call | flops 2000000000 | bytes 5000000 | tf_op jit(solution)/shard_map/pallas_call | solution.py:862
  94.2 2.3 %shard_map.154 = (bf16[16,16,384]{2,1,0:T(8,128)(2,1)}, bf16[16,16,384]{2,1,0:T(8,128)(2,1)}, bf16[192,1536]{1,0:T(8,128)(2,1)}, f32[3,225]{1,0:T(4,128)}, f32[3]{0:T(128)}, /*index=5*/f32[384]{0:T(512)}, f32[384]{0:T(512)}) custom-call(bf16[4,4,16,384]{3,2,1,0:T(8,128)(2,1)} %get-tuple-element.18.blocks_f, ...), custom_call_target="tpu_custom_call" | custom-call | flops 1000000 | bytes 2000000 | tf_op jit(solution)/shard_map/pallas_call | solution.py:889
